TPU v7x, 512 devices: a whole 4x4x16 slice. The times are simulated.
512 devices in a mesh: rep: 32 (over z_lo, x, core), fsdp: 16 (over y, z_hi).
Axes of the slice: x: 4, y: 4, z: 16 (z_hi: 4, z_lo: 4; z = z_hi * 4 + z_lo), core: 2. Of those that a mesh axis runs over, the one named last changes fastest.
Arguments:
- tokens: bfloat16 [32, 4096, 7168], P('rep', 'fsdp'), may hold values from -6 to 6
- cotangent: bfloat16 [32, 4096, 112], P('rep', 'fsdp'), may hold values from -6 to 6
- params: float32 [32, 802816], P('rep', 'fsdp'), may hold values from -0.0625 to 0.0625
- first_moment: float32 [32, 802816], P('rep', 'fsdp'), may hold values from -30 to 30
- second_moment: float32 [32, 802816], P('rep', 'fsdp'), may hold values from 100 to 1000
- mass: float32 [32], P('rep'), may hold values from 0.5 to 2
- step_index: int32 [1], replicated, may hold values from 0 to 999
Outputs:
- new_params: float32 [32, 802816], P('rep', 'fsdp')
- new_first: float32 [32, 802816], P('rep', 'fsdp')
- new_second: float32 [32, 802816], P('rep', 'fsdp')
- new_mass: float32 [32], P('rep')
All inputs are finite; a program needn't handle non-finite values.
Results may differ from a plain program's by a relative error of at most 0.017.
Values may be sent and summed in bfloat16 or wider, within the bound.
No kernel may reach another device: no remote copies, remote signals or barrier semaphores. Data moves between devices by JAX's collectives and lax.ppermute only.
A program may use at most 64 MiB of HBM per device.

v0:
```python
import functools

import jax
import jax.numpy as jnp
from jax import lax
from jax.experimental import pallas as pl
from jax.experimental.pallas import tpu as pltpu
from jax.sharding import PartitionSpec as P

D = 7168
HEAD = 112
STEPS = 2
TOK = 256
NY = 4
NZ = 4
QUARTER = D // NY
SHARD_ROWS = QUARTER // NZ
LANES = 128
FLAT = SHARD_ROWS * HEAD // LANES
WIRE = FLAT + 8
GROUPS = SHARD_ROWS // 8
BLOCK = QUARTER + LANES

BETA_ONE = 0.9
BETA_TWO = 0.95
ADAM_EPS = 1e-08
RATE = 0.01

F32 = jnp.float32
BF16 = jnp.bfloat16
VMEM = pl.BlockSpec(memory_space=pltpu.VMEM)
SMEM = pl.BlockSpec(memory_space=pltpu.SMEM)
PARAMS = pltpu.CompilerParams(vmem_limit_bytes=40 * 1024 * 1024)

Z_GROUPS = [[y * NZ + z for z in range(NZ)] for y in range(NY)]
Y_GROUPS = [[y * NZ + z for y in range(NY)] for z in range(NZ)]


def shape(dims, dtype):
    return jax.ShapeDtypeStruct(dims, dtype)


def y_shift(array, by):
    pairs = [(y * NZ + z, (y + by) % NY * NZ + z) for y in range(NY) for z in range(NZ)]
    return lax.ppermute(array, "fsdp", pairs)


def gossip(array, distance):
    count = lax.axis_size("rep")
    return lax.ppermute(array, "rep", [(i, (i + distance) % count) for i in range(count)])


def lanes_of(rows):
    return lax.broadcasted_iota(jnp.int32, (rows, LANES), 1)


def flat_to_rows(flat, base, rows):
    lane = lanes_of(GROUPS)
    for j in range(8):
        if j == 0:
            part = flat[pl.ds(base, GROUPS, stride=7), :]
        else:
            part = flat[pl.ds(base + j - 1, GROUPS, stride=7), :]
            if j < 7:
                after = flat[pl.ds(base + j, GROUPS, stride=7), :]
                part = jnp.where(lane < LANES - 16 * j, after, part)
            part = pltpu.roll(part, 16 * j, 1)
        rows[pl.ds(j, GROUPS, stride=8), :] = jnp.where(lane < HEAD, part, 0.0)


def rows_to_flat(rows, base, flat):
    lane = lanes_of(GROUPS)
    for i in range(7):
        first = rows[pl.ds(base + i, GROUPS, stride=8), :]
        second = rows[pl.ds(base + i + 1, GROUPS, stride=8), :]
        if i:
            first = pltpu.roll(first, LANES - 16 * i, 1)
        second = pltpu.roll(second, HEAD - 16 * i, 1)
        flat[pl.ds(i, GROUPS, stride=7), :] = jnp.where(lane < HEAD - 16 * i, first, second)


def norm_kernel(place, tokens, cotangent, *outs):
    values = tokens[...].astype(F32)
    center = jnp.mean(values, axis=-1, keepdims=True)
    spread = jnp.mean((values - center) ** 2, axis=-1, keepdims=True)
    scale = lax.rsqrt(spread + 1e-05)
    cot = jnp.concatenate(
        [cotangent[...], jnp.zeros((LANES - HEAD, cotangent.shape[1]), BF16)], axis=0
    ).T
    for k, out in enumerate(outs):
        start = pl.multiple_of((place[0] + k) % NY * QUARTER, LANES)
        part = tokens[:, pl.ds(start, QUARTER)].astype(F32)
        out[:, :QUARTER] = ((part - center) * scale).astype(BF16)
        out[:, QUARTER:] = cot


def norm(place, tokens, cotangent):
    rows = 128
    return pl.pallas_call(
        norm_kernel,
        grid=(TOK // rows,),
        in_specs=[
            SMEM,
            pl.BlockSpec((rows, D), lambda i: (i, 0)),
            pl.BlockSpec((HEAD, rows), lambda i: (0, i)),
        ],
        out_specs=[pl.BlockSpec((rows, BLOCK), lambda i: (i, 0))] * NY,
        out_shape=[shape((TOK, BLOCK), BF16)] * NY,
        compiler_params=PARAMS,
        name="norm",
    )(place, tokens, cotangent)


def start_kernel(mass, params, own, wire):
    own[:FLAT, :] = params[...]
    own[FLAT:, :] = jnp.full((WIRE - FLAT, LANES), mass[0], F32)
    wire[...] = (own[...] / mass[0]).astype(BF16)


def start(mass, params):
    return pl.pallas_call(
        start_kernel,
        in_specs=[SMEM, VMEM],
        out_specs=[VMEM] * 2,
        out_shape=[shape((WIRE, LANES), F32), shape((WIRE, LANES), BF16)],
        compiler_params=PARAMS,
        name="start",
    )(mass, params)


def preact_kernel(place, wires, *refs):
    blocks, (out, flat, rows, weights) = refs[:NY], refs[NY:]
    flat[...] = wires[...].astype(F32)
    for s in range(NZ):
        flat_to_rows(flat, s * WIRE, rows)
        weights[pl.ds(s * SHARD_ROWS, SHARD_ROWS), :] = rows[...].astype(BF16)
    for k, block in enumerate(blocks):
        product = jnp.dot(block[:, :QUARTER], weights[...], preferred_element_type=F32)
        start = pl.multiple_of((place[0] + NY - k) % NY * TOK, TOK)
        out[pl.ds(start, TOK), :] = product[:, :HEAD].astype(BF16)


def partial_preact(place, wires, blocks):
    return pl.pallas_call(
        preact_kernel,
        in_specs=[SMEM] + [VMEM] * (1 + NY),
        out_specs=VMEM,
        out_shape=shape((NY * TOK, HEAD), BF16),
        scratch_shapes=[
            pltpu.VMEM((NZ * WIRE, LANES), F32),
            pltpu.VMEM((SHARD_ROWS, LANES), F32),
            pltpu.VMEM((QUARTER, LANES), BF16),
        ],
        compiler_params=PARAMS,
        name="partial_preact",
    )(place, wires, *blocks)


def grad_kernel(place, partials, *refs):
    blocks, (out, heads, rows, flat) = refs[:NY], refs[NY:]
    heads[...] = jnp.zeros_like(heads)
    total = jnp.zeros((LANES, QUARTER), F32)
    for k, block in enumerate(blocks):
        start = pl.multiple_of((place[0] + NY - k) % NY * TOK, TOK)
        preact = jnp.zeros((TOK, HEAD), F32)
        for s in range(NY):
            preact = preact + partials[pl.ds(s * NY * TOK + start, TOK), :].astype(F32)
        cot = block[:, QUARTER:QUARTER + HEAD].astype(F32)
        sig = 1.0 / (1.0 + jnp.exp(-preact))
        heads[:, :HEAD] = (cot * sig * (1.0 + preact * (1.0 - sig))).astype(BF16)
        total = total + lax.dot_general(
            heads[...], block[:, :QUARTER], (((0,), (0,)), ((), ())), preferred_element_type=F32
        )
    rows[...] = total.T
    flat[FLAT:, :] = jnp.zeros((WIRE - FLAT, LANES), F32)
    for s in range(NZ):
        rows_to_flat(rows, s * SHARD_ROWS, flat)
        out[s] = flat[...].astype(BF16)


def quarter_grad(place, partials, blocks):
    return pl.pallas_call(
        grad_kernel,
        in_specs=[SMEM] + [VMEM] * (1 + NY),
        out_specs=VMEM,
        out_shape=shape((NZ, WIRE, LANES), BF16),
        scratch_shapes=[
            pltpu.VMEM((TOK, LANES), BF16),
            pltpu.VMEM((QUARTER, LANES), F32),
            pltpu.VMEM((WIRE, LANES), F32),
        ],
        compiler_params=PARAMS,
        name="quarter_grad",
    )(place, partials, *blocks)


def adam(section, scales, terms, first_moment, second_moment, own, peer):
    grads = terms[0].astype(F32)
    for s in range(1, NZ):
        grads = grads + terms[s].astype(F32)
    grads = grads[:FLAT, :]
    first = BETA_ONE * first_moment[...] + (1.0 - BETA_ONE) * grads
    second = BETA_TWO * second_moment[...] + (1.0 - BETA_TWO) * grads * grads
    update = first / scales[2 * section] / (jnp.sqrt(second / scales[2 * section + 1]) + ADAM_EPS)
    mixed = 0.5 * (own[...] + peer[...])
    return first, second, mixed[:FLAT, :] - RATE * update, mixed[FLAT:, :]


def between_kernel(scales, terms, first_moment, second_moment, own, peer, *outs):
    new_first, new_second, new_own, wire = outs
    first, second, params, mass = adam(
        0, scales, terms, first_moment, second_moment, own, peer
    )
    new_first[...] = first
    new_second[...] = second
    new_own[:FLAT, :] = params
    new_own[FLAT:, :] = mass
    wire[...] = (new_own[...] / mass[0:1, :]).astype(BF16)


def between(scales, terms, first_moment, second_moment, own, peer):
    return pl.pallas_call(
        between_kernel,
        in_specs=[SMEM] + [VMEM] * 5,
        out_specs=[VMEM] * 4,
        out_shape=[
            shape((FLAT, LANES), F32),
            shape((FLAT, LANES), F32),
            shape((WIRE, LANES), F32),
            shape((WIRE, LANES), BF16),
        ],
        compiler_params=PARAMS,
        name="between",
    )(scales, terms, first_moment, second_moment, own, peer)


def last_kernel(scales, terms, first_moment, second_moment, own, peer, *outs):
    new_params, new_first, new_second, new_mass = outs
    first, second, params, mass = adam(
        1, scales, terms, first_moment, second_moment, own, peer
    )
    new_first[...] = first
    new_second[...] = second
    new_params[...] = params
    new_mass[0] = mass[0, 0]


def last(scales, terms, first_moment, second_moment, own, peer):
    return pl.pallas_call(
        last_kernel,
        in_specs=[SMEM] + [VMEM] * 5,
        out_specs=[VMEM] * 3 + [SMEM],
        out_shape=[shape((FLAT, LANES), F32)] * 3 + [shape((1,), F32)],
        compiler_params=PARAMS,
        name="last",
    )(scales, terms, first_moment, second_moment, own, peer)


def exchange(distance, partial, own):
    peer = gossip(own, distance)
    partials = lax.all_gather(partial, "fsdp", axis=0, tiled=True, axis_index_groups=Y_GROUPS)
    return partials, peer


def on_device(tokens, cotangent, params, first_moment, second_moment, mass, step_index):
    levels = lax.axis_size("rep").bit_length() - 1
    counts = (step_index[0] + 1 + jnp.arange(STEPS)).astype(F32)
    scales = jnp.stack(
        [1.0 - jnp.power(BETA_ONE, counts), 1.0 - jnp.power(BETA_TWO, counts)], axis=1
    ).reshape(-1)
    place = (lax.axis_index("fsdp") // NZ).astype(jnp.int32).reshape(1)
    first_moment = first_moment.reshape(FLAT, LANES)
    second_moment = second_moment.reshape(FLAT, LANES)
    own, wire = start(mass, params.reshape(FLAT, LANES))
    picks = [(step_index[0] + section) % levels for section in range(STEPS)]
    wire, scales, *picks = lax.optimization_barrier((wire, scales, *picks))
    blocks = norm(place, tokens[0], cotangent[0].T)
    blocks = [blocks[0]] + [y_shift(blocks[k], k) for k in range(1, NY)]
    for section in range(STEPS):
        wires = lax.all_gather(wire, "fsdp", axis=0, tiled=True, axis_index_groups=Z_GROUPS)
        partial = partial_preact(place, wires, blocks)
        partials, peer = lax.switch(
            picks[section],
            [functools.partial(exchange, 2**level) for level in range(levels)],
            partial, own,
        )
        terms = quarter_grad(place, partials, blocks)
        terms = lax.all_to_all(terms, "fsdp", 0, 0, axis_index_groups=Z_GROUPS)
        if section < STEPS - 1:
            first_moment, second_moment, own, wire = between(
                scales, terms, first_moment, second_moment, own, peer
            )
    *new, new_mass = last(scales, terms, first_moment, second_moment, own, peer)
    return tuple(array.reshape(1, -1) for array in new) + (new_mass,)


def solution(mesh):
    placed = (
        P("rep", "fsdp", None),
        P("rep", "fsdp", None),
        P("rep", "fsdp"),
        P("rep", "fsdp"),
        P("rep", "fsdp"),
        P("rep"),
        P(),
    )
    return jax.shard_map(
        on_device,
        mesh=mesh,
        in_specs=placed,
        out_specs=(P("rep", "fsdp"), P("rep", "fsdp"), P("rep", "fsdp"), P("rep")),
        check_vma=False,
    )
```

profile of v0, /device:TPU:6, one launch (start us, length us, event | category | flops | bytes accessed | tf_op | source)
XLA Modules:
  0.0 203.9 jit_solution(6474193817164645273)
XLA Ops:
  0.6 0.0 copy-start
  0.7 2.0 copy-done
  2.7 0.8 copy-done.9
  3.5 0.0 copy-start.2
  3.5 4.6 %norm.1 = (bf16[256,1920]{1,0:T(8,128)(2,1)S(1)}, bf16[256,1920]{1,0:T(8,128)(2,1)}, bf16[256,1920]{1,0:T(8,128)(2,1)}, bf16[256,1920]{1,0:T(8,128)(2,1)}) custom-call(s32[1]{0:T(128)} %bitcast.3.place, bf16[256,7168]{1,0:T(8,128)(2,1)S(1)} %bitcast.13, bf16[112,256]{1,0:T(8,128)(2,1)S(1)} %bitcast.17), custom_call_target="tpu_custom_call" | custom-call | tf_op jit(solution)/shard_map/norm/pallas_call | solution.py:99
  8.1 3.5 %collective-permute-start.10 = (bf16[256,1920]{1,0:T(8,128)(2,1)}, bf16[256,1920]{1,0:T(8,128)(2,1)S(1)}, u32[]{:S(2)}, u32[]{:S(2)}) collective-permute-start(bf16[256,1920]{1,0:T(8,128)(2,1)} %get-tuple-element.92), channel_id=1, source_target_pairs={{0,4},{1,5},{2,6},{3,7},{4,8},{5,9},{6,10},{7,11},{8,12},{9,13},{1... | collective-permute-start | bytes 2949128 | tf_op jit(solution)/shard_map/ppermute | solution.py:45
  11.6 4.8 %collective-permute-start.11 = (bf16[256,1920]{1,0:T(8,128)(2,1)}, bf16[256,1920]{1,0:T(8,128)(2,1)S(1)}, u32[]{:S(2)}, u32[]{:S(2)}) collective-permute-start(bf16[256,1920]{1,0:T(8,128)(2,1)} %get-tuple-element.93), channel_id=1, source_target_pairs={{0,8},{1,9},{2,10},{3,11},{4,12},{5,13},{6,14},{7,15},{8,0},{9,1},... | collective-permute-start | bytes 2949128 | tf_op jit(solution)/shard_map/ppermute | solution.py:45
  16.4 3.3 %collective-permute-start.12 = (bf16[256,1920]{1,0:T(8,128)(2,1)}, bf16[256,1920]{1,0:T(8,128)(2,1)}, u32[]{:S(2)}, u32[]{:S(2)}) collective-permute-start(bf16[256,1920]{1,0:T(8,128)(2,1)} %get-tuple-element.94), channel_id=1, source_target_pairs={{0,12},{1,13},{2,14},{3,15},{4,0},{5,1},{6,2},{7,3},{8,4},{9,5},{1... | collective-permute-start | bytes 2949128 | tf_op jit(solution)/shard_map/ppermute | solution.py:45
  21.0 0.1 pad_maximum_fusion
  21.1 0.1 reshape.60.scales
  21.2 0.0 copy-done.2
  21.2 0.7 start.1
  21.9 30.4 %all_gather.36.wires = bf16[1600,128]{1,0:T(8,128)(2,1)S(1)} all-gather(bf16[400,128]{1,0:T(8,128)(2,1)S(1)} %get-tuple-element.90), channel_id=1, replica_groups={{0,1,2,3},{4,5,6,7},{8,9,10,11},{12,13,14,15},{16,17,18,19},{20,21,22,2..., dimensions={0}, use_global_device_ids=true | all-gather | bytes 512000 | tf_op jit(solution)/shard_map/all_gather | solution.py:280
  52.3 0.0 collective-permute-done.10.refs_1_
  52.3 5.0 %collective-permute-done.11.refs_2_ = bf16[256,1920]{1,0:T(8,128)(2,1)S(1)} collective-permute-done((bf16[256,1920]{1,0:T(8,128)(2,1)}, bf16[256,1920]{1,0:T(8,128)(2,1)S(1)}, u32[]{:S(2)}, u32[]{:S(2)}) %collective-permute-start.11) | collective-permute-done | bytes 983072 | tf_op jit(solution)/shard_map/ppermute | solution.py:45
  57.2 1.5 collective-permute-done.12.refs_3_
  58.7 2.5 %partial_preact.2 = bf16[1024,112]{1,0:T(8,128)(2,1)S(1)} custom-call(s32[1]{0:T(128)} %bitcast.3.place, bf16[1600,128]{1,0:T(8,128)(2,1)S(1)} %all_gather.36.wires, bf16[256,1920]{1,0:T(8,128)(2,1)S(1)} %get-tuple-element.91.refs_0_, bf16[256,1920]{1,0:T(8,128)(2,1)S(1)} %collective-permute-done.10.refs_1_, ...), custom_call_target="tpu_custom_call" | custom-call | tf_op jit(solution)/shard_map/partial_preact/pallas_call | solution.py:144
  61.2 17.4 %conditional.2 = (bf16[4096,112]{1,0:T(8,128)(2,1)S(1)}, f32[400,128]{1,0:T(8,128)}) conditional(s32[]{:T(128)} %clamp.7, (bf16[1024,112]{1,0:T(8,128)(2,1)S(1)}, f32[400,128]{1,0:T(8,128)}) %tuple.50, (bf16[1024,112]{1,0:T(8,128)(2,1)S(1)}, f32[400,128]{1,0:T(8,128)}) %tuple.50, (bf16[1024,112]{1,0:T(8,128)(2,1)S(1)}, ...), branch_computations={%region_0.1_spmd, %region_1.2_spmd, %region_2.3_spmd, %region_3.4_... | conditional | bytes 1966136 | solution.py:282
  61.2 1.9 collective-permute-start
  63.1 15.4 %all_gather.24 = bf16[4096,112]{1,0:T(8,128)(2,1)S(1)} all-gather(bf16[1024,112]{1,0:T(8,128)(2,1)S(1)} %get-tuple-element.40), channel_id=1, replica_groups={{0,4,8,12},{1,5,9,13},{2,6,10,14},{3,7,11,15},{16,20,24,28},{17,21,25,2..., dimensions={0}, use_global_device_ids=true | all-gather | bytes 1146880 | tf_op jit(solution)/shard_map/cond/branch_0_fun/all_gather | solution.py:261
  78.6 0.0 collective-permute-done
  78.6 0.0 copy-start.10
  78.6 1.0 copy-done.10
  79.5 3.1 %quarter_grad.2 = bf16[4,400,128]{2,1,0:T(8,128)(2,1)S(1)} custom-call(s32[1]{0:T(128)} %bitcast.3.place, bf16[4096,112]{1,0:T(8,128)(2,1)} %copy-done.10, bf16[256,1920]{1,0:T(8,128)(2,1)S(1)} %get-tuple-element.91.refs_0_, bf16[256,1920]{1,0:T(8,128)(2,1)S(1)} %collective-permute-done.10.refs_1_, bf16[256,1920]{1,0:T(8,128)(2,1)S(1)} %collective-permute-done.11.refs_2_, ...), custom_call_target="tpu_custom_call" | custom-call | tf_op jit(solution)/shard_map/quarter_grad/pallas_call | solution.py:182
  82.6 0.0 copy-start.1
  82.7 0.7 copy-done.1
  83.4 15.3 %all-to-all-start = ((bf16[4,400,128]{2,1,0:T(8,128)(2,1)}), bf16[4,400,128]{2,1,0:T(8,128)(2,1)S(1)}, u32[]{:S(2)}, u32[]{:S(2)}) async-start(bf16[4,400,128]{2,1,0:T(8,128)(2,1)} %copy-done.1), calls=%async_computation | async-start | bytes 819200 | tf_op jit(solution)/shard_map/all_to_all | solution.py:288
  98.7 20.8 %all-to-all-done.terms = bf16[4,400,128]{2,1,0:T(8,128)(2,1)S(1)} async-done(((bf16[4,400,128]{2,1,0:T(8,128)(2,1)}), bf16[4,400,128]{2,1,0:T(8,128)(2,1)S(1)}, u32[]{:S(2)}, u32[]{:S(2)}) %all-to-all-start) | async-done | bytes 409632 | tf_op jit(solution)/shard_map/all_to_all | solution.py:288
  119.5 0.0 copy-start.3
  119.5 0.9 copy-done.3
  120.5 0.0 copy-start.4
  120.5 0.9 copy-done.4
  121.4 2.0 between.1
  123.4 0.0 copy-start.5
  123.4 0.7 copy-done.5
  124.1 0.7 copy-done.7
  124.7 25.3 %all_gather.37.wires = bf16[1600,128]{1,0:T(8,128)(2,1)S(1)} all-gather(bf16[400,128]{1,0:T(8,128)(2,1)S(1)} %get-tuple-element.98), channel_id=1, replica_groups={{0,1,2,3},{4,5,6,7},{8,9,10,11},{12,13,14,15},{16,17,18,19},{20,21,22,2..., dimensions={0}, use_global_device_ids=true | all-gather | bytes 512000 | tf_op jit(solution)/shard_map/all_gather | solution.py:280
  150.0 2.5 %partial_preact.3 = bf16[1024,112]{1,0:T(8,128)(2,1)S(1)} custom-call(s32[1]{0:T(128)} %bitcast.3.place, bf16[1600,128]{1,0:T(8,128)(2,1)S(1)} %all_gather.37.wires, bf16[256,1920]{1,0:T(8,128)(2,1)S(1)} %get-tuple-element.91.refs_0_, bf16[256,1920]{1,0:T(8,128)(2,1)S(1)} %collective-permute-done.10.refs_1_, ...), custom_call_target="tpu_custom_call" | custom-call | tf_op jit(solution)/shard_map/partial_preact/pallas_call | solution.py:144
  152.5 20.0 %conditional.3 = (bf16[4096,112]{1,0:T(8,128)(2,1)}, f32[400,128]{1,0:T(8,128)}) conditional(s32[]{:T(128)} %clamp.6, (bf16[1024,112]{1,0:T(8,128)(2,1)S(1)}, f32[400,128]{1,0:T(8,128)}) %tuple.51, (bf16[1024,112]{1,0:T(8,128)(2,1)S(1)}, f32[400,128]{1,0:T(8,128)}) %tuple.51, (bf16[1024,112]{1,0:T(8,128)(2,1)S(1)}, ...), branch_computations={%region_5.6_spmd, %region_6.7_spmd, %region_7.8_spmd, %region_8.9_... | conditional | bytes 1966136 | solution.py:282
  152.6 4.3 %collective-permute-start.6 = (f32[400,128]{1,0:T(8,128)}, f32[400,128]{1,0:T(8,128)}, u32[]{:S(2)}, u32[]{:S(2)}) collective-permute-start(f32[400,128]{1,0:T(8,128)} %get-tuple-element.53), channel_id=1, source_target_pairs={{0,32},{16,48},{32,64},{48,80},{64,96},{80,112},{96,128},{112,144}... | collective-permute-start | bytes 614408 | tf_op jit(solution)/shard_map/cond/branch_1_fun/ppermute | solution.py:50
  156.8 15.7 %all_gather.30 = bf16[4096,112]{1,0:T(8,128)(2,1)} all-gather(bf16[1024,112]{1,0:T(8,128)(2,1)S(1)} %get-tuple-element.52), channel_id=1, replica_groups={{0,4,8,12},{1,5,9,13},{2,6,10,14},{3,7,11,15},{16,20,24,28},{17,21,25,2..., dimensions={0}, use_global_device_ids=true | all-gather | bytes 1146880 | tf_op jit(solution)/shard_map/cond/branch_1_fun/all_gather | solution.py:261
  172.5 0.0 collective-permute-done.6
  172.5 0.0 copy-start.8
  172.5 3.1 %quarter_grad.3 = bf16[4,400,128]{2,1,0:T(8,128)(2,1)S(1)} custom-call(s32[1]{0:T(128)} %bitcast.3.place, bf16[4096,112]{1,0:T(8,128)(2,1)} %get-tuple-element.100.partials, bf16[256,1920]{1,0:T(8,128)(2,1)S(1)} %get-tuple-element.91.refs_0_, bf16[256,1920]{1,0:T(8,128)(2,1)S(1)} %collective-permute-done.10.refs_1_, ...), custom_call_target="tpu_custom_call" | custom-call | tf_op jit(solution)/shard_map/quarter_grad/pallas_call | solution.py:182
  175.7 26.2 %all_to_all.10.terms = bf16[4,400,128]{2,1,0:T(8,128)(2,1)S(1)} all-to-all(bf16[4,400,128]{2,1,0:T(8,128)(2,1)S(1)} %quarter_grad.3), channel_id=1, replica_groups={{0,1,2,3},{4,5,6,7},{8,9,10,11},{12,13,14,15},{16,17,18,19},{20,21,22,2..., dimensions={0} | all-to-all | bytes 819200 | tf_op jit(solution)/shard_map/all_to_all | solution.py:288
  201.9 0.0 copy-done.6
  201.9 0.0 copy-done.8
  201.9 2.0 last.1
  (4 shorter events, 0.0 us)
Async XLA Ops:
  0.6 2.0 %copy-start = (bf16[1,256,7168]{2,1,0:T(8,128)(2,1)S(1)}, bf16[1,256,7168]{2,1,0:T(8,128)(2,1)}, u32[]{:S(2)}) copy-start(bf16[1,256,7168]{2,1,0:T(8,128)(2,1)} %param.17) | copy-start | bytes 11010052
  2.7 0.8 copy-start.9
  3.5 17.7 %copy-start.2 = (f32[1,50176]{1,0:T(1,128)S(1)}, f32[1,50176]{1,0:T(1,128)}, u32[]{:S(2)}) copy-start(f32[1,50176]{1,0:T(1,128)} %param.19) | copy-start | bytes 602116
  8.1 44.1 %collective-permute-start.10 = (bf16[256,1920]{1,0:T(8,128)(2,1)}, bf16[256,1920]{1,0:T(8,128)(2,1)S(1)}, u32[]{:S(2)}, u32[]{:S(2)}) collective-permute-start(bf16[256,1920]{1,0:T(8,128)(2,1)} %get-tuple-element.92), channel_id=1, source_target_pairs={{0,4},{1,5},{2,6},{3,7},{4,8},{5,9},{6,10},{7,11},{8,12},{9,13},{1... | collective-permute-start | bytes 2949128 | tf_op jit(solution)/shard_map/ppermute | solution.py:45
  11.6 45.6 %collective-permute-start.11 = (bf16[256,1920]{1,0:T(8,128)(2,1)}, bf16[256,1920]{1,0:T(8,128)(2,1)S(1)}, u32[]{:S(2)}, u32[]{:S(2)}) collective-permute-start(bf16[256,1920]{1,0:T(8,128)(2,1)} %get-tuple-element.93), channel_id=1, source_target_pairs={{0,8},{1,9},{2,10},{3,11},{4,12},{5,13},{6,14},{7,15},{8,0},{9,1},... | collective-permute-start | bytes 2949128 | tf_op jit(solution)/shard_map/ppermute | solution.py:45
  16.4 42.3 %collective-permute-start.12 = (bf16[256,1920]{1,0:T(8,128)(2,1)}, bf16[256,1920]{1,0:T(8,128)(2,1)}, u32[]{:S(2)}, u32[]{:S(2)}) collective-permute-start(bf16[256,1920]{1,0:T(8,128)(2,1)} %get-tuple-element.94), channel_id=1, source_target_pairs={{0,12},{1,13},{2,14},{3,15},{4,0},{5,1},{6,2},{7,3},{8,4},{9,5},{1... | collective-permute-start | bytes 2949128 | tf_op jit(solution)/shard_map/ppermute | solution.py:45
  61.2 17.3 %collective-permute-start = (f32[400,128]{1,0:T(8,128)}, f32[400,128]{1,0:T(8,128)}, u32[]{:S(2)}, u32[]{:S(2)}) collective-permute-start(f32[400,128]{1,0:T(8,128)} %get-tuple-element.41), channel_id=1, source_target_pairs={{0,16},{16,32},{32,48},{48,64},{64,80},{80,96},{96,112},{112,128},... | collective-permute-start | bytes 614408 | tf_op jit(solution)/shard_map/cond/branch_0_fun/ppermute | solution.py:50
  78.6 1.0 copy-start.10
  82.6 0.8 copy-start.1
  83.4 36.1 %all-to-all-start = ((bf16[4,400,128]{2,1,0:T(8,128)(2,1)}), bf16[4,400,128]{2,1,0:T(8,128)(2,1)S(1)}, u32[]{:S(2)}, u32[]{:S(2)}) async-start(bf16[4,400,128]{2,1,0:T(8,128)(2,1)} %copy-done.1), calls=%async_computation | async-start | bytes 819200 | tf_op jit(solution)/shard_map/all_to_all | solution.py:288
  119.5 0.9 copy-start.3
  120.5 0.9 copy-start.4
  123.4 0.7 copy-start.5
  124.1 0.7 copy-start.7
  152.6 19.9 %collective-permute-start.6 = (f32[400,128]{1,0:T(8,128)}, f32[400,128]{1,0:T(8,128)}, u32[]{:S(2)}, u32[]{:S(2)}) collective-permute-start(f32[400,128]{1,0:T(8,128)} %get-tuple-element.53), channel_id=1, source_target_pairs={{0,32},{16,48},{32,64},{48,80},{64,96},{80,112},{96,128},{112,144}... | collective-permute-start | bytes 614408 | tf_op jit(solution)/shard_map/cond/branch_1_fun/ppermute | solution.py:50
  172.5 29.4 %copy-start.6 = (f32[392,128]{1,0:T(8,128)S(1)}, f32[392,128]{1,0:T(8,128)}, u32[]{:S(2)}) copy-start(f32[392,128]{1,0:T(8,128)} %copy-done.5) | copy-start | bytes 602116
  172.5 29.4 %copy-start.8 = (f32[392,128]{1,0:T(8,128)S(1)}, f32[392,128]{1,0:T(8,128)}, u32[]{:S(2)}) copy-start(f32[392,128]{1,0:T(8,128)} %copy-done.7) | copy-start | bytes 602116
where the time goes:
time: 205 us; the launch traced here: 204 us
  blocking collectives  113 us (55%)
  starting transfers between devices  33 us (16%)
  waiting for transfers between devices  27.3 us (13%)
  Pallas kernels  20.6 us (10%)
  local copies, waits for them, and re-layouts  7.9 us (4%)
  between operations  2.06 us (1%)
    all_gather x2, blocking collectives, on_device(): lax.all_gather(wire, 'fsdp', axis=0, tiled=True, axis_index_groups=Z_GROUPS)  55.7 us
    all_gather x2, blocking collectives, exchange(): lax.all_gather(partial, 'fsdp', axis=0, tiled=True, axis_index_groups=Y_G...  31.1 us
    all_to_all x1, blocking collectives, on_device(): terms = lax.all_to_all(terms, 'fsdp', 0, 0, axis_index_groups=Z_GROUPS)  26.2 us
    all_to_all x1, waiting for transfers between devices, on_device(): terms = lax.all_to_all(terms, 'fsdp', 0, 0, axis_index_groups=Z_GROUPS)  20.8 us
    all_to_all x1, starting transfers between devices, on_device(): terms = lax.all_to_all(terms, 'fsdp', 0, 0, axis_index_groups=Z_GROUPS)  15.3 us
    ppermute x3, starting transfers between devices, y_shift(): return lax.ppermute(array, 'fsdp', pairs)  11.5 us
    unnamed x22, local copies, waits for them, and re-layouts  7.81 us
    ppermute x3, waiting for transfers between devices, y_shift(): return lax.ppermute(array, 'fsdp', pairs)  6.42 us
  transfers between devices with their start and end apart: 6, of which 3 were waited for; matrix products, arithmetic and copies ran while one was open for 0% of the time, Pallas kernels for 0%

commit v1 on v0

v1 whole, which is shorter than its diff:
```python
import functools

import jax
import jax.numpy as jnp
from jax import lax
from jax.experimental import pallas as pl
from jax.experimental.pallas import tpu as pltpu
from jax.sharding import PartitionSpec as P

D = 7168
HEAD = 112
STEPS = 2
TOK = 256
NY = 4
NZ = 4
QUARTER = D // NY
SHARD_ROWS = QUARTER // NZ
LANES = 128
FLAT = SHARD_ROWS * HEAD // LANES
WIRE = FLAT + 8
GROUPS = SHARD_ROWS // 8
BLOCK = QUARTER + LANES
CHUNKS = 4
CHUNK = TOK // CHUNKS

BETA_ONE = 0.9
BETA_TWO = 0.95
ADAM_EPS = 1e-08
RATE = 0.01

F32 = jnp.float32
BF16 = jnp.bfloat16
VMEM = pl.BlockSpec(memory_space=pltpu.VMEM)
SMEM = pl.BlockSpec(memory_space=pltpu.SMEM)
HBM = pl.BlockSpec(memory_space=pltpu.HBM)
DMA = pltpu.SemaphoreType.DMA
PARAMS = pltpu.CompilerParams(vmem_limit_bytes=40 * 1024 * 1024)

Z_GROUPS = [[y * NZ + z for z in range(NZ)] for y in range(NY)]
Y_GROUPS = [[y * NZ + z for y in range(NY)] for z in range(NZ)]


def in_hbm(array):
    return pltpu.with_memory_space_constraint(array, pltpu.HBM)


def shape(dims, dtype):
    return jax.ShapeDtypeStruct(dims, dtype)


def y_shift(array, by):
    pairs = [(y * NZ + z, (y + by) % NY * NZ + z) for y in range(NY) for z in range(NZ)]
    return lax.ppermute(array, "fsdp", pairs)


def gossip(array, distance):
    count = lax.axis_size("rep")
    return lax.ppermute(array, "rep", [(i, (i + distance) % count) for i in range(count)])


def lanes_of(rows):
    return lax.broadcasted_iota(jnp.int32, (rows, LANES), 1)


def flat_to_rows(flat, base, rows):
    lane = lanes_of(GROUPS)
    for j in range(8):
        if j == 0:
            part = flat[pl.ds(base, GROUPS, stride=7), :]
        else:
            part = flat[pl.ds(base + j - 1, GROUPS, stride=7), :]
            if j < 7:
                after = flat[pl.ds(base + j, GROUPS, stride=7), :]
                part = jnp.where(lane < LANES - 16 * j, after, part)
            part = pltpu.roll(part, 16 * j, 1)
        rows[pl.ds(j, GROUPS, stride=8), :] = jnp.where(lane < HEAD, part, 0.0)


def rows_to_flat(rows, base, flat):
    lane = lanes_of(GROUPS)
    for i in range(7):
        first = rows[pl.ds(base + i, GROUPS, stride=8), :]
        second = rows[pl.ds(base + i + 1, GROUPS, stride=8), :]
        if i:
            first = pltpu.roll(first, LANES - 16 * i, 1)
        second = pltpu.roll(second, HEAD - 16 * i, 1)
        flat[pl.ds(i, GROUPS, stride=7), :] = jnp.where(lane < HEAD - 16 * i, first, second)


def norm_kernel(place, tokens, cotangent, *refs):
    (own, *far), (values, cot, near, sems, out_sems) = refs[:NY], refs[NY:]
    chunks = [pl.ds(i * CHUNK, CHUNK) for i in range(CHUNKS)]
    copies = [
        pltpu.make_async_copy(tokens.at[rows], values.at[rows], sems.at[i])
        for i, rows in enumerate(chunks)
    ]
    copies.append(pltpu.make_async_copy(cotangent, cot, sems.at[CHUNKS]))
    for copy in (copies[-1], *copies[:-1]):
        copy.start()
    outs = [own, *(near.at[k] for k in range(NY - 1))]
    copies[-1].wait()
    padded = jnp.concatenate([cot[...], jnp.zeros((LANES - HEAD, TOK), BF16)], axis=0).T
    for out in outs:
        out[:, QUARTER:] = padded
    sent = []
    for i, rows in enumerate(chunks):
        copies[i].wait()
        totals = [jnp.zeros((CHUNK, LANES), F32) for _ in range(4)]
        for c in range(D // LANES):
            totals[c % 4] += values[rows, c * LANES:(c + 1) * LANES].astype(F32)
        center = jnp.sum(sum(totals), axis=-1, keepdims=True) * (1.0 / D)
        center = jnp.broadcast_to(center, (CHUNK, LANES))
        totals = [jnp.zeros((CHUNK, LANES), F32) for _ in range(2)]
        for c in range(D // LANES):
            apart = values[rows, c * LANES:(c + 1) * LANES].astype(F32) - center
            totals[c % 2] += apart * apart
        spread = jnp.sum(sum(totals), axis=-1, keepdims=True) * (1.0 / D)
        scale = jnp.broadcast_to(lax.rsqrt(spread + 1e-05), (CHUNK, LANES))
        for k in (*range(1, NY), 0):
            start = (place[0] + k) % NY * QUARTER
            for c in range(QUARTER // LANES):
                lanes = pl.ds(pl.multiple_of(start + c * LANES, LANES), LANES)
                part = (values[rows, lanes].astype(F32) - center) * scale
                outs[k][rows, c * LANES:(c + 1) * LANES] = part.astype(BF16)
            if k:
                sent.append(
                    pltpu.make_async_copy(
                        near.at[k - 1, rows], far[k - 1].at[rows], out_sems.at[i, k - 1]
                    )
                )
                sent[-1].start()
    for copy in sent:
        copy.wait()


def norm(place, tokens, cotangent):
    return pl.pallas_call(
        norm_kernel,
        in_specs=[SMEM, HBM, HBM],
        out_specs=[VMEM] + [HBM] * (NY - 1),
        out_shape=[shape((TOK, BLOCK), BF16)] + [pltpu.HBM((TOK, BLOCK), BF16)] * (NY - 1),
        scratch_shapes=[
            pltpu.VMEM((TOK, D), BF16),
            pltpu.VMEM((HEAD, TOK), BF16),
            pltpu.VMEM((NY - 1, TOK, BLOCK), BF16),
            DMA((CHUNKS + 1,)),
            DMA((CHUNKS, NY - 1)),
        ],
        compiler_params=PARAMS,
        name="norm",
    )(place, in_hbm(tokens), in_hbm(cotangent))


def start_kernel(mass, params, own, wire):
    own[:FLAT, :] = params[...]
    own[FLAT:, :] = jnp.full((WIRE - FLAT, LANES), mass[0], F32)
    wire[...] = (own[...] / mass[0]).astype(BF16)


def start(mass, params):
    return pl.pallas_call(
        start_kernel,
        in_specs=[SMEM, VMEM],
        out_specs=[VMEM] * 2,
        out_shape=[shape((WIRE, LANES), F32), shape((WIRE, LANES), BF16)],
        compiler_params=PARAMS,
        name="start",
    )(mass, params)


def preact_kernel(place, wires, *refs):
    blocks, (out, flat, rows, weights, held, sem) = refs[:NY], refs[NY:]
    fetch = pltpu.make_async_copy(blocks[-1], held, sem)
    fetch.start()
    flat[...] = wires[...].astype(F32)
    for s in range(NZ):
        flat_to_rows(flat, s * WIRE, rows)
        weights[pl.ds(s * SHARD_ROWS, SHARD_ROWS), :] = rows[...].astype(BF16)
    for k, block in enumerate((*blocks[:-1], held)):
        if block is held:
            fetch.wait()
        product = jnp.dot(block[:, :QUARTER], weights[...], preferred_element_type=F32)
        start = pl.multiple_of((place[0] + NY - k) % NY * TOK, TOK)
        out[pl.ds(start, TOK), :] = product[:, :HEAD].astype(BF16)


def partial_preact(place, wires, blocks):
    return pl.pallas_call(
        preact_kernel,
        in_specs=[SMEM] + [VMEM] * NY + [HBM],
        out_specs=VMEM,
        out_shape=shape((NY * TOK, HEAD), BF16),
        scratch_shapes=[
            pltpu.VMEM((NZ * WIRE, LANES), F32),
            pltpu.VMEM((SHARD_ROWS, LANES), F32),
            pltpu.VMEM((QUARTER, LANES), BF16),
            pltpu.VMEM((TOK, BLOCK), BF16),
            DMA,
        ],
        compiler_params=PARAMS,
        name="partial_preact",
    )(place, wires, *blocks[:-1], in_hbm(blocks[-1]))


def grad_kernel(near, place, partials, *refs):
    blocks, refs = refs[:NY], refs[NY:]
    if near:
        states, (out, near_first, near_second, mixed), refs = refs[:4], refs[4:8], refs[8:]
        heads, rows, flat, held, near_peer, sems = refs
        pairs = [(blocks[-1], held), *zip(states, (near_first, near_second, mixed, near_peer))]
    else:
        out, heads, rows, flat, held, sems = refs
        pairs = [(blocks[-1], held)]
    copies = [
        pltpu.make_async_copy(source, into, sems.at[i]) for i, (source, into) in enumerate(pairs)
    ]
    for copy in copies:
        copy.start()
    heads[...] = jnp.zeros_like(heads)
    total = jnp.zeros((LANES, QUARTER), F32)
    for k, block in enumerate((*blocks[:-1], held)):
        start = pl.multiple_of((place[0] + NY - k) % NY * TOK, TOK)
        preact = jnp.zeros((TOK, HEAD), F32)
        for s in range(NY):
            preact = preact + partials[pl.ds(s * NY * TOK + start, TOK), :].astype(F32)
        if block is held:
            copies[0].wait()
        cot = block[:, QUARTER:QUARTER + HEAD].astype(F32)
        sig = 1.0 / (1.0 + jnp.exp(-preact))
        heads[:, :HEAD] = (cot * sig * (1.0 + preact * (1.0 - sig))).astype(BF16)
        total = total + lax.dot_general(
            heads[...], block[:, :QUARTER], (((0,), (0,)), ((), ())), preferred_element_type=F32
        )
    rows[...] = total.T
    flat[FLAT:, :] = jnp.zeros((WIRE - FLAT, LANES), F32)
    for s in range(NZ):
        rows_to_flat(rows, s * SHARD_ROWS, flat)
        out[s] = flat[...].astype(BF16)
    if near:
        for copy in copies[1:]:
            copy.wait()
        mixed[...] = 0.5 * (mixed[...] + near_peer[...])


def quarter_grad(place, partials, blocks, *states):
    near = bool(states)
    return pl.pallas_call(
        functools.partial(grad_kernel, near),
        in_specs=[SMEM] + [VMEM] * NY + [HBM] * (1 + len(states)),
        out_specs=[VMEM] * (4 if near else 1),
        out_shape=[
            shape((NZ, WIRE, LANES), BF16),
            shape((FLAT, LANES), F32),
            shape((FLAT, LANES), F32),
            shape((WIRE, LANES), F32),
        ][:4 if near else 1],
        scratch_shapes=[
            pltpu.VMEM((TOK, LANES), BF16),
            pltpu.VMEM((QUARTER, LANES), F32),
            pltpu.VMEM((WIRE, LANES), F32),
            pltpu.VMEM((TOK, BLOCK), BF16),
            *[pltpu.VMEM((WIRE, LANES), F32)] * near,
            DMA((1 + len(states),)),
        ],
        compiler_params=PARAMS,
        name="quarter_grad",
    )(place, partials, *blocks[:-1], in_hbm(blocks[-1]), *map(in_hbm, states))


def adam(section, scales, terms, first_moment, second_moment, mixed):
    grads = terms[0].astype(F32)
    for s in range(1, NZ):
        grads = grads + terms[s].astype(F32)
    grads = grads[:FLAT, :]
    first = BETA_ONE * first_moment[...] + (1.0 - BETA_ONE) * grads
    second = BETA_TWO * second_moment[...] + (1.0 - BETA_TWO) * grads * grads
    update = first / scales[2 * section] / (jnp.sqrt(second / scales[2 * section + 1]) + ADAM_EPS)
    return first, second, mixed[:FLAT, :] - RATE * update, mixed[FLAT:, :]


def between_kernel(scales, terms, *refs):
    states, (far_first, far_second, new_own, wire), refs = refs[:4], refs[4:8], refs[8:]
    first_moment, second_moment, own, peer, new_first, new_second, sems = refs
    pairs = [
        *zip(states, (first_moment, second_moment, own, peer)),
        (new_first, far_first), (new_second, far_second),
    ]
    copies = [
        pltpu.make_async_copy(source, into, sems.at[i]) for i, (source, into) in enumerate(pairs)
    ]
    for copy in copies[:4]:
        copy.start()
    for copy in copies[:4]:
        copy.wait()
    own[...] = 0.5 * (own[...] + peer[...])
    first, second, params, mass = adam(0, scales, terms, first_moment, second_moment, own)
    new_first[...] = first
    new_second[...] = second
    for copy in copies[4:]:
        copy.start()
    new_own[:FLAT, :] = params
    new_own[FLAT:, :] = mass
    wire[...] = (new_own[...] / mass[0:1, :]).astype(BF16)
    for copy in copies[4:]:
        copy.wait()


def between(scales, terms, *states):
    flat, wide = pltpu.VMEM((FLAT, LANES), F32), pltpu.VMEM((WIRE, LANES), F32)
    return pl.pallas_call(
        between_kernel,
        in_specs=[SMEM, VMEM] + [HBM] * 4,
        out_specs=[HBM] * 2 + [VMEM] * 2,
        out_shape=[
            pltpu.HBM((FLAT, LANES), F32),
            pltpu.HBM((FLAT, LANES), F32),
            shape((WIRE, LANES), F32),
            shape((WIRE, LANES), BF16),
        ],
        scratch_shapes=[flat, flat, wide, wide, flat, flat, DMA((6,))],
        compiler_params=PARAMS,
        name="between",
    )(scales, terms, *map(in_hbm, states))


def last_kernel(scales, terms, first_moment, second_moment, mixed, *outs):
    new_params, new_first, new_second, new_mass = outs
    first, second, params, mass = adam(1, scales, terms, first_moment, second_moment, mixed)
    new_first[...] = first
    new_second[...] = second
    new_params[...] = params
    new_mass[0] = mass[0, 0]


def last(scales, *arrays):
    return pl.pallas_call(
        last_kernel,
        in_specs=[SMEM] + [VMEM] * 4,
        out_specs=[VMEM] * 3 + [SMEM],
        out_shape=[shape((FLAT, LANES), F32)] * 3 + [shape((1,), F32)],
        compiler_params=PARAMS,
        name="last",
    )(scales, *arrays)


def gather(array, groups):
    return lax.all_gather(array, "fsdp", axis=0, tiled=True, axis_index_groups=groups)


def gossip_alone(distance, own):
    return gossip(own, distance)


def gossip_beside(distance, own, wire):
    return gossip(own, distance), gather(wire, Z_GROUPS)


def at_level(pick, levels, function, *operands):
    return lax.switch(
        pick, [functools.partial(function, 2**level) for level in range(levels)], *operands
    )


def on_device(tokens, cotangent, params, first_moment, second_moment, mass, step_index):
    levels = lax.axis_size("rep").bit_length() - 1
    counts = (step_index[0] + 1 + jnp.arange(STEPS)).astype(F32)
    scales = jnp.stack(
        [1.0 - jnp.power(BETA_ONE, counts), 1.0 - jnp.power(BETA_TWO, counts)], axis=1
    ).reshape(-1)
    picks = [(step_index[0] + section) % levels for section in range(STEPS)]
    place = (lax.axis_index("fsdp") // NZ).astype(jnp.int32).reshape(1)
    first_moment = first_moment.reshape(FLAT, LANES)
    second_moment = second_moment.reshape(FLAT, LANES)
    own, wire = start(mass, params.reshape(FLAT, LANES))
    wire, scales, *picks = lax.optimization_barrier((wire, scales, *picks))
    blocks = norm(place, tokens[0], cotangent[0].T)
    blocks = [blocks[0]] + [y_shift(blocks[k], k) for k in range(1, NY)]
    for section in range(STEPS):
        if section == 0:
            wires = gather(wire, Z_GROUPS)
            wires, own = lax.optimization_barrier((wires, own))
            peer = at_level(picks[section], levels, gossip_alone, own)
            wires, peer = lax.optimization_barrier((wires, peer))
        else:
            peer, wires = at_level(picks[section], levels, gossip_beside, own, wire)
        partials = gather(partial_preact(place, wires, blocks), Y_GROUPS)
        states = first_moment, second_moment, own, peer
        terms, *near = quarter_grad(place, partials, blocks, *(states if section else ()))
        terms = lax.all_to_all(terms, "fsdp", 0, 0, axis_index_groups=Z_GROUPS)
        terms, *picks = lax.optimization_barrier((terms, *picks))
        if section < STEPS - 1:
            first_moment, second_moment, own, wire = between(scales, terms, *states)
    *new, new_mass = last(scales, terms, *near)
    return tuple(array.reshape(1, -1) for array in new) + (new_mass,)


def solution(mesh):
    placed = (
        P("rep", "fsdp", None),
        P("rep", "fsdp", None),
        P("rep", "fsdp"),
        P("rep", "fsdp"),
        P("rep", "fsdp"),
        P("rep"),
        P(),
    )
    return jax.shard_map(
        on_device,
        mesh=mesh,
        in_specs=placed,
        out_specs=(P("rep", "fsdp"), P("rep", "fsdp"), P("rep", "fsdp"), P("rep")),
        check_vma=False,
    )
```

time: 205 us -> 196 us (0.956)
  blocking collectives: 113 us -> 146 us
  waiting for transfers between devices: 27.3 us -> 7.85 us
  starting transfers between devices: 33 us -> 19.7 us
  local copies, waits for them, and re-layouts: 7.9 us -> 0.09 us
    all_to_all x1 -> x2, blocking collectives: 26.2 us -> 65.2 us  [on_device(): terms = lax.all_to_all(terms, 'fsdp', 0, 0, axis_index_groups=Z_GROUPS)]
    all_to_all x1 -> x0, waiting for transfers between devices: 20.8 us -> none  [on_device(): terms = lax.all_to_all(terms, 'fsdp', 0, 0, axis_index_groups=Z_GROUPS)]
    all_to_all x1 -> x0, starting transfers between devices: 15.3 us -> none  [on_device(): terms = lax.all_to_all(terms, 'fsdp', 0, 0, axis_index_groups=Z_GROUPS)]
    ppermute x2, waiting for transfers between devices: 0.01 us -> 7.84 us  [gossip(): lax.ppermute(array, 'rep', [(i, (i + distance) % count) for i in range(co...]
    unnamed x22 -> x2, local copies, waits for them, and re-layouts: 7.81 us -> 0.01 us
    ppermute x3, waiting for transfers between devices: 6.42 us -> 0.01 us  [y_shift(): return lax.ppermute(array, 'fsdp', pairs)]
    all_gather x4, blocking collectives: 86.7 us -> 80.7 us  [gather(): lax.all_gather(array, 'fsdp', axis=0, tiled=True, axis_index_groups=groups)]
  transfers between devices with their start and end apart: 6 -> 5, of which waited for: 3 -> 1; matrix products, arithmetic and copies ran while one was open for 0% -> 0% of each run, Pallas kernels for 0% -> 0%
where the time goes in v1:
time: 196 us; the launch traced here: 195 us
  blocking collectives  146 us (74%)
  starting transfers between devices  19.7 us (10%)
  Pallas kernels  19.3 us (10%)
  waiting for transfers between devices  7.85 us (4%)
  between operations  2.06 us (1%)
    all_gather x4, blocking collectives, gather(): lax.all_gather(array, 'fsdp', axis=0, tiled=True, axis_index_groups=groups)  80.7 us
    all_to_all x2, blocking collectives, on_device(): terms = lax.all_to_all(terms, 'fsdp', 0, 0, axis_index_groups=Z_GROUPS)  65.2 us
    ppermute x3, starting transfers between devices, y_shift(): return lax.ppermute(array, 'fsdp', pairs)  11.6 us
    ppermute x2, starting transfers between devices, gossip(): lax.ppermute(array, 'rep', [(i, (i + distance) % count) for i in range(co...  8.16 us
    ppermute x2, waiting for transfers between devices, gossip(): lax.ppermute(array, 'rep', [(i, (i + distance) % count) for i in range(co...  7.84 us
    pallas_call x2, Pallas kernels, quarter_grad(): pl.pallas_call(functools.partial(grad_kernel, near), in_specs=[SMEM] + [V...  4.96 us
    pallas_call x1, Pallas kernels, norm(): pl.pallas_call(norm_kernel, in_specs=[SMEM, HBM, HBM], out_specs=[VMEM] +...  4.48 us
    pallas_call x2, Pallas kernels, partial_preact(): pl.pallas_call(preact_kernel, in_specs=[SMEM] + [VMEM] * NY + [HBM], out_...  4.23 us
  transfers between devices with their start and end apart: 5, of which 1 were waited for; matrix products, arithmetic and copies ran while one was open for 0% of the time, Pallas kernels for 0%

profile of v1, /device:TPU:6, one launch (start us, length us, event | category | flops | bytes accessed | tf_op | source)
XLA Modules:
  0.0 195.0 jit_solution(516905629142115581)
XLA Ops:
  0.6 0.0 copy-start
  0.7 4.5 %norm.1 = (bf16[256,1920]{1,0:T(8,128)(2,1)S(1)}, bf16[256,1920]{1,0:T(8,128)(2,1)}, bf16[256,1920]{1,0:T(8,128)(2,1)}, bf16[256,1920]{1,0:T(8,128)(2,1)}) custom-call(s32[1]{0:T(128)} %bitcast.3.place, bf16[256,7168]{1,0:T(8,128)(2,1)} %bitcast.14, bf16[112,256]{1,0:T(8,128)(2,1)} %bitcast.17), custom_call_target="tpu_custom_call" | custom-call | tf_op jit(solution)/shard_map/norm/pallas_call | solution.py:137
  5.1 3.5 %collective-permute-start.10 = (bf16[256,1920]{1,0:T(8,128)(2,1)}, bf16[256,1920]{1,0:T(8,128)(2,1)S(1)}, u32[]{:S(2)}, u32[]{:S(2)}) collective-permute-start(bf16[256,1920]{1,0:T(8,128)(2,1)} %get-tuple-element.85), channel_id=1, source_target_pairs={{0,4},{1,5},{2,6},{3,7},{4,8},{5,9},{6,10},{7,11},{8,12},{9,13},{1... | collective-permute-start | bytes 2949128 | tf_op jit(solution)/shard_map/ppermute | solution.py:53
  8.6 4.8 %collective-permute-start.11 = (bf16[256,1920]{1,0:T(8,128)(2,1)}, bf16[256,1920]{1,0:T(8,128)(2,1)S(1)}, u32[]{:S(2)}, u32[]{:S(2)}) collective-permute-start(bf16[256,1920]{1,0:T(8,128)(2,1)} %get-tuple-element.86), channel_id=1, source_target_pairs={{0,8},{1,9},{2,10},{3,11},{4,12},{5,13},{6,14},{7,15},{8,0},{9,1},... | collective-permute-start | bytes 2949128 | tf_op jit(solution)/shard_map/ppermute | solution.py:53
  13.5 3.3 %collective-permute-start.12 = (bf16[256,1920]{1,0:T(8,128)(2,1)}, bf16[256,1920]{1,0:T(8,128)(2,1)}, u32[]{:S(2)}, u32[]{:S(2)}) collective-permute-start(bf16[256,1920]{1,0:T(8,128)(2,1)} %get-tuple-element.87), channel_id=1, source_target_pairs={{0,12},{1,13},{2,14},{3,15},{4,0},{5,1},{6,2},{7,3},{8,4},{9,5},{1... | collective-permute-start | bytes 2949128 | tf_op jit(solution)/shard_map/ppermute | solution.py:53
  18.1 0.1 pad_maximum_fusion
  18.1 0.1 reshape.60.scales
  18.2 0.0 copy-done
  18.2 0.7 start.1
  18.9 30.4 %all_gather.24.wires = bf16[1600,128]{1,0:T(8,128)(2,1)S(1)} all-gather(bf16[400,128]{1,0:T(8,128)(2,1)S(1)} %get-tuple-element.78), channel_id=1, replica_groups={{0,1,2,3},{4,5,6,7},{8,9,10,11},{12,13,14,15},{16,17,18,19},{20,21,22,2..., dimensions={0}, use_global_device_ids=true | all-gather | bytes 512000 | tf_op jit(solution)/shard_map/all_gather | solution.py:347
  49.3 9.8 %conditional.2 = (f32[400,128]{1,0:T(8,128)}) conditional(s32[]{:T(128)} %clamp.6, f32[400,128]{1,0:T(8,128)} %get-tuple-element.82.refs_2_, f32[400,128]{1,0:T(8,128)} %get-tuple-element.82.refs_2_, f32[400,128]{1,0:T(8,128)} %get-tuple-element.82.refs_2_, f32[400,128]{1,0:T(8,128)} %get-tuple-element.82.refs_2_, ...), branch_computations={%region_0.1_spmd, %region_1.2_spmd, %region_2.3_spmd, %region_3.4_... | conditional | bytes 819248 | solution.py:359
  49.3 1.9 collective-permute-start.3
  51.2 7.8 %collective-permute-done.3 = f32[400,128]{1,0:T(8,128)} collective-permute-done((f32[400,128]{1,0:T(8,128)}, f32[400,128]{1,0:T(8,128)}, u32[]{:S(2)}, u32[]{:S(2)}) %collective-permute-start.3) | collective-permute-done | bytes 204832 | tf_op jit(solution)/shard_map/cond/branch_3_fun/ppermute | solution.py:58
  59.0 0.0 collective-permute-done.10.refs_1_
  59.1 0.0 collective-permute-done.11.refs_2_
  59.1 0.0 collective-permute-done.12.refs_3_
  59.1 2.1 %partial_preact.2 = bf16[1024,112]{1,0:T(8,128)(2,1)S(1)} custom-call(s32[1]{0:T(128)} %bitcast.3.place, bf16[1600,128]{1,0:T(8,128)(2,1)S(1)} %all_gather.24.wires, bf16[256,1920]{1,0:T(8,128)(2,1)S(1)} %get-tuple-element.84.refs_0_, bf16[256,1920]{1,0:T(8,128)(2,1)S(1)} %collective-permute-done.10.refs_1_, ...), custom_call_target="tpu_custom_call" | custom-call | tf_op jit(solution)/shard_map/partial_preact/pallas_call | solution.py:188
  61.2 15.2 %all_gather.25.partials = bf16[4096,112]{1,0:T(8,128)(2,1)S(1)} all-gather(bf16[1024,112]{1,0:T(8,128)(2,1)S(1)} %partial_preact.2), channel_id=1, replica_groups={{0,4,8,12},{1,5,9,13},{2,6,10,14},{3,7,11,15},{16,20,24,28},{17,21,25,2..., dimensions={0}, use_global_device_ids=true | all-gather | bytes 1146880 | tf_op jit(solution)/shard_map/all_gather | solution.py:347
  76.4 2.3 %quarter_grad.2 = bf16[4,400,128]{2,1,0:T(8,128)(2,1)S(1)} custom-call(s32[1]{0:T(128)} %bitcast.3.place, bf16[4096,112]{1,0:T(8,128)(2,1)S(1)} %all_gather.25.partials, bf16[256,1920]{1,0:T(8,128)(2,1)S(1)} %get-tuple-element.84.refs_0_, bf16[256,1920]{1,0:T(8,128)(2,1)S(1)} %collective-permute-done.10.refs_1_, ...), custom_call_target="tpu_custom_call" | custom-call | tf_op jit(solution)/shard_map/quarter_grad/pallas_call | solution.py:247
  78.7 34.8 %all_to_all.10.terms = bf16[4,400,128]{2,1,0:T(8,128)(2,1)S(1)} all-to-all(bf16[4,400,128]{2,1,0:T(8,128)(2,1)S(1)} %quarter_grad.2), channel_id=1, replica_groups={{0,1,2,3},{4,5,6,7},{8,9,10,11},{12,13,14,15},{16,17,18,19},{20,21,22,2..., dimensions={0} | all-to-all | bytes 819200 | tf_op jit(solution)/shard_map/all_to_all | solution.py:389
  113.5 3.4 %between.1 = (f32[392,128]{1,0:T(8,128)}, f32[392,128]{1,0:T(8,128)}, f32[400,128]{1,0:T(8,128)}, bf16[400,128]{1,0:T(8,128)(2,1)S(1)}) custom-call(f32[4]{0:T(128)S(1)} %reshape.60.scales, bf16[4,400,128]{2,1,0:T(8,128)(2,1)S(1)} %all_to_all.10.terms, f32[392,128]{1,0:T(8,128)} %bitcast.15, f32[392,128]{1,0:T(8,128)} %bitcast.16, ...), custom_call_target="tpu_custom_call" | custom-call | tf_op jit(solution)/shard_map/between/pallas_call | solution.py:310
  116.9 27.6 %conditional.3 = (f32[400,128]{1,0:T(8,128)}, bf16[1600,128]{1,0:T(8,128)(2,1)S(1)}) conditional(s32[]{:T(128)} %clamp.7, (f32[400,128]{1,0:T(8,128)}, bf16[400,128]{1,0:T(8,128)(2,1)S(1)}) %tuple.53, (f32[400,128]{1,0:T(8,128)}, bf16[400,128]{1,0:T(8,128)(2,1)S(1)}) %tuple.53, (f32[400,128]{1,0:T(8,128)}, ...), branch_computations={%region_5.6_spmd, %region_6.7_spmd, %region_7.8_spmd, %region_8.9_... | conditional | bytes 1331256 | solution.py:359
  117.0 6.2 %collective-permute-start.9 = (f32[400,128]{1,0:T(8,128)}, f32[400,128]{1,0:T(8,128)}, u32[]{:S(2)}, u32[]{:S(2)}) collective-permute-start(f32[400,128]{1,0:T(8,128)} %get-tuple-element.39), channel_id=1, source_target_pairs={{0,256},{16,272},{32,288},{48,304},{64,320},{80,336},{96,352},{112... | collective-permute-start | bytes 614408 | tf_op jit(solution)/shard_map/cond/branch_4_fun/ppermute | solution.py:58
  123.2 21.3 %all_gather.20 = bf16[1600,128]{1,0:T(8,128)(2,1)S(1)} all-gather(bf16[400,128]{1,0:T(8,128)(2,1)S(1)} %get-tuple-element.40), channel_id=1, replica_groups={{0,1,2,3},{4,5,6,7},{8,9,10,11},{12,13,14,15},{16,17,18,19},{20,21,22,2..., dimensions={0}, use_global_device_ids=true | all-gather | bytes 512000 | tf_op jit(solution)/shard_map/cond/branch_4_fun/all_gather | solution.py:347
  144.5 0.0 collective-permute-done.9
  144.5 2.1 %partial_preact.3 = bf16[1024,112]{1,0:T(8,128)(2,1)S(1)} custom-call(s32[1]{0:T(128)} %bitcast.3.place, bf16[1600,128]{1,0:T(8,128)(2,1)S(1)} %get-tuple-element.94.wires, bf16[256,1920]{1,0:T(8,128)(2,1)S(1)} %get-tuple-element.84.refs_0_, bf16[256,1920]{1,0:T(8,128)(2,1)S(1)} %collective-permute-done.10.refs_1_, ...), custom_call_target="tpu_custom_call" | custom-call | tf_op jit(solution)/shard_map/partial_preact/pallas_call | solution.py:188
  146.6 13.8 %all_gather.26.partials = bf16[4096,112]{1,0:T(8,128)(2,1)S(1)} all-gather(bf16[1024,112]{1,0:T(8,128)(2,1)S(1)} %partial_preact.3), channel_id=1, replica_groups={{0,4,8,12},{1,5,9,13},{2,6,10,14},{3,7,11,15},{16,20,24,28},{17,21,25,2..., dimensions={0}, use_global_device_ids=true | all-gather | bytes 1146880 | tf_op jit(solution)/shard_map/all_gather | solution.py:347
  160.5 2.7 %quarter_grad.3 = (bf16[4,400,128]{2,1,0:T(8,128)(2,1)S(1)}, f32[392,128]{1,0:T(8,128)S(1)}, f32[392,128]{1,0:T(8,128)S(1)}, f32[400,128]{1,0:T(8,128)S(1)}) custom-call(s32[1]{0:T(128)} %bitcast.3.place, bf16[4096,112]{1,0:T(8,128)(2,1)S(1)} %all_gather.26.partials, bf16[256,1920]{1,0:T(8,128)(2,1)S(1)} %get-tuple-element.84.refs_0_, ...), custom_call_target="tpu_custom_call" | custom-call | tf_op jit(solution)/shard_map/quarter_grad/pallas_call | solution.py:247
  163.1 30.4 %all_to_all.11.terms = bf16[4,400,128]{2,1,0:T(8,128)(2,1)S(1)} all-to-all(bf16[4,400,128]{2,1,0:T(8,128)(2,1)S(1)} %get-tuple-element.98), channel_id=1, replica_groups={{0,1,2,3},{4,5,6,7},{8,9,10,11},{12,13,14,15},{16,17,18,19},{20,21,22,2..., dimensions={0} | all-to-all | bytes 819200 | tf_op jit(solution)/shard_map/all_to_all | solution.py:389
  193.5 1.5 last.1
  (1 shorter events, 0.0 us)
Async XLA Ops:
  0.6 17.6 %copy-start = (f32[1,50176]{1,0:T(1,128)S(1)}, f32[1,50176]{1,0:T(1,128)}, u32[]{:S(2)}) copy-start(f32[1,50176]{1,0:T(1,128)} %param.19) | copy-start | bytes 602116
  5.1 53.9 %collective-permute-start.10 = (bf16[256,1920]{1,0:T(8,128)(2,1)}, bf16[256,1920]{1,0:T(8,128)(2,1)S(1)}, u32[]{:S(2)}, u32[]{:S(2)}) collective-permute-start(bf16[256,1920]{1,0:T(8,128)(2,1)} %get-tuple-element.85), channel_id=1, source_target_pairs={{0,4},{1,5},{2,6},{3,7},{4,8},{5,9},{6,10},{7,11},{8,12},{9,13},{1... | collective-permute-start | bytes 2949128 | tf_op jit(solution)/shard_map/ppermute | solution.py:53
  8.6 50.4 %collective-permute-start.11 = (bf16[256,1920]{1,0:T(8,128)(2,1)}, bf16[256,1920]{1,0:T(8,128)(2,1)S(1)}, u32[]{:S(2)}, u32[]{:S(2)}) collective-permute-start(bf16[256,1920]{1,0:T(8,128)(2,1)} %get-tuple-element.86), channel_id=1, source_target_pairs={{0,8},{1,9},{2,10},{3,11},{4,12},{5,13},{6,14},{7,15},{8,0},{9,1},... | collective-permute-start | bytes 2949128 | tf_op jit(solution)/shard_map/ppermute | solution.py:53
  13.5 45.6 %collective-permute-start.12 = (bf16[256,1920]{1,0:T(8,128)(2,1)}, bf16[256,1920]{1,0:T(8,128)(2,1)}, u32[]{:S(2)}, u32[]{:S(2)}) collective-permute-start(bf16[256,1920]{1,0:T(8,128)(2,1)} %get-tuple-element.87), channel_id=1, source_target_pairs={{0,12},{1,13},{2,14},{3,15},{4,0},{5,1},{6,2},{7,3},{8,4},{9,5},{1... | collective-permute-start | bytes 2949128 | tf_op jit(solution)/shard_map/ppermute | solution.py:53
  49.3 9.8 %collective-permute-start.3 = (f32[400,128]{1,0:T(8,128)}, f32[400,128]{1,0:T(8,128)}, u32[]{:S(2)}, u32[]{:S(2)}) collective-permute-start(f32[400,128]{1,0:T(8,128)} %param.3), channel_id=1, source_target_pairs={{0,128},{16,144},{32,160},{48,176},{64,192},{80,208},{96,224},{112... | collective-permute-start | bytes 614408 | tf_op jit(solution)/shard_map/cond/branch_3_fun/ppermute | solution.py:58
  117.0 27.6 %collective-permute-start.9 = (f32[400,128]{1,0:T(8,128)}, f32[400,128]{1,0:T(8,128)}, u32[]{:S(2)}, u32[]{:S(2)}) collective-permute-start(f32[400,128]{1,0:T(8,128)} %get-tuple-element.39), channel_id=1, source_target_pairs={{0,256},{16,272},{32,288},{48,304},{64,320},{80,336},{96,352},{112... | collective-permute-start | bytes 614408 | tf_op jit(solution)/shard_map/cond/branch_4_fun/ppermute | solution.py:58

commit v2 on v1

--- a/solution.py
+++ b/solution.py
@@ -22,6 +22,10 @@
 BLOCK = QUARTER + LANES
 CHUNKS = 4
 CHUNK = TOK // CHUNKS
+HALF = TOK // 2
+EARLY = ((2, 0, HALF),)
+LATER = ((2, HALF, HALF), (1, 0, TOK), (3, 0, TOK), (0, 0, TOK))
+PARTS = (LATER[3], LATER[1], EARLY[0], LATER[0], LATER[2])
 
 BETA_ONE = 0.9
 BETA_TWO = 0.95
@@ -87,21 +91,25 @@
         flat[pl.ds(i, GROUPS, stride=7), :] = jnp.where(lane < HEAD - 16 * i, first, second)
 
 
-def norm_kernel(place, tokens, cotangent, *refs):
-    (own, *far), (values, cot, near, sems, out_sems) = refs[:NY], refs[NY:]
-    chunks = [pl.ds(i * CHUNK, CHUNK) for i in range(CHUNKS)]
+def norm_kernel(parts, rows_in, place, tokens, cotangent, *refs):
+    outs, refs = refs[:len(parts)], refs[len(parts):]
+    values, cot, sems, out_sems, *nears = refs
+    chunks = [pl.ds(i * CHUNK, CHUNK) for i in range(rows_in // CHUNK)]
     copies = [
         pltpu.make_async_copy(tokens.at[rows], values.at[rows], sems.at[i])
         for i, rows in enumerate(chunks)
     ]
-    copies.append(pltpu.make_async_copy(cotangent, cot, sems.at[CHUNKS]))
+    copies.append(
+        pltpu.make_async_copy(cotangent.at[:, pl.ds(0, rows_in)], cot, sems.at[len(chunks)])
+    )
     for copy in (copies[-1], *copies[:-1]):
         copy.start()
-    outs = [own, *(near.at[k] for k in range(NY - 1))]
     copies[-1].wait()
-    padded = jnp.concatenate([cot[...], jnp.zeros((LANES - HEAD, TOK), BF16)], axis=0).T
-    for out in outs:
-        out[:, QUARTER:] = padded
+    padded = jnp.concatenate([cot[...], jnp.zeros((LANES - HEAD, rows_in), BF16)], axis=0).T
+    held = []
+    for out, (k, first, count) in zip(outs, parts):
+        held.append(nears.pop(0) if k else out)
+        held[-1][:, QUARTER:] = padded[first:first + count]
     sent = []
     for i, rows in enumerate(chunks):
         copies[i].wait()
@@ -116,16 +124,19 @@
             totals[c % 2] += apart * apart
         spread = jnp.sum(sum(totals), axis=-1, keepdims=True) * (1.0 / D)
         scale = jnp.broadcast_to(lax.rsqrt(spread + 1e-05), (CHUNK, LANES))
-        for k in (*range(1, NY), 0):
+        for n, (k, first, count) in enumerate(parts):
+            if not first <= i * CHUNK < first + count:
+                continue
+            into = pl.ds(i * CHUNK - first, CHUNK)
             start = (place[0] + k) % NY * QUARTER
             for c in range(QUARTER // LANES):
                 lanes = pl.ds(pl.multiple_of(start + c * LANES, LANES), LANES)
                 part = (values[rows, lanes].astype(F32) - center) * scale
-                outs[k][rows, c * LANES:(c + 1) * LANES] = part.astype(BF16)
+                held[n][into, c * LANES:(c + 1) * LANES] = part.astype(BF16)
             if k:
                 sent.append(
                     pltpu.make_async_copy(
-                        near.at[k - 1, rows], far[k - 1].at[rows], out_sems.at[i, k - 1]
+                        held[n].at[into], outs[n].at[into], out_sems.at[n, i]
                     )
                 )
                 sent[-1].start()
@@ -133,18 +144,21 @@
         copy.wait()
 
 
-def norm(place, tokens, cotangent):
-    return pl.pallas_call(
-        norm_kernel,
+def norm(parts, rows_in, place, tokens, cotangent):
+    return pl.pallas_call(
+        functools.partial(norm_kernel, parts, rows_in),
         in_specs=[SMEM, HBM, HBM],
-        out_specs=[VMEM] + [HBM] * (NY - 1),
-        out_shape=[shape((TOK, BLOCK), BF16)] + [pltpu.HBM((TOK, BLOCK), BF16)] * (NY - 1),
+        out_specs=[HBM if k else VMEM for k, _, _ in parts],
+        out_shape=[
+            pltpu.HBM((count, BLOCK), BF16) if k else shape((count, BLOCK), BF16)
+            for k, _, count in parts
+        ],
         scratch_shapes=[
-            pltpu.VMEM((TOK, D), BF16),
-            pltpu.VMEM((HEAD, TOK), BF16),
-            pltpu.VMEM((NY - 1, TOK, BLOCK), BF16),
-            DMA((CHUNKS + 1,)),
-            DMA((CHUNKS, NY - 1)),
+            pltpu.VMEM((rows_in, D), BF16),
+            pltpu.VMEM((HEAD, rows_in), BF16),
+            DMA((rows_in // CHUNK + 1,)),
+            DMA((len(parts), rows_in // CHUNK)),
+            *[pltpu.VMEM((count, BLOCK), BF16) for k, _, count in parts if k],
         ],
         compiler_params=PARAMS,
         name="norm",
@@ -169,32 +183,32 @@
 
 
 def preact_kernel(place, wires, *refs):
-    blocks, (out, flat, rows, weights, held, sem) = refs[:NY], refs[NY:]
+    blocks, (out, flat, rows, weights, held, sem) = refs[:len(PARTS)], refs[len(PARTS):]
     fetch = pltpu.make_async_copy(blocks[-1], held, sem)
     fetch.start()
     flat[...] = wires[...].astype(F32)
     for s in range(NZ):
         flat_to_rows(flat, s * WIRE, rows)
         weights[pl.ds(s * SHARD_ROWS, SHARD_ROWS), :] = rows[...].astype(BF16)
-    for k, block in enumerate((*blocks[:-1], held)):
+    for block, (k, first, count) in zip((*blocks[:-1], held), PARTS):
         if block is held:
             fetch.wait()
         product = jnp.dot(block[:, :QUARTER], weights[...], preferred_element_type=F32)
-        start = pl.multiple_of((place[0] + NY - k) % NY * TOK, TOK)
-        out[pl.ds(start, TOK), :] = product[:, :HEAD].astype(BF16)
+        start = pl.multiple_of((place[0] + NY - k) % NY * TOK + first, HALF)
+        out[pl.ds(start, count), :] = product[:, :HEAD].astype(BF16)
 
 
 def partial_preact(place, wires, blocks):
     return pl.pallas_call(
         preact_kernel,
-        in_specs=[SMEM] + [VMEM] * NY + [HBM],
+        in_specs=[SMEM] + [VMEM] * len(PARTS) + [HBM],
         out_specs=VMEM,
         out_shape=shape((NY * TOK, HEAD), BF16),
         scratch_shapes=[
             pltpu.VMEM((NZ * WIRE, LANES), F32),
             pltpu.VMEM((SHARD_ROWS, LANES), F32),
             pltpu.VMEM((QUARTER, LANES), BF16),
-            pltpu.VMEM((TOK, BLOCK), BF16),
+            pltpu.VMEM((PARTS[-1][2], BLOCK), BF16),
             DMA,
         ],
         compiler_params=PARAMS,
@@ -203,7 +217,7 @@
 
 
 def grad_kernel(near, place, partials, *refs):
-    blocks, refs = refs[:NY], refs[NY:]
+    blocks, refs = refs[:len(PARTS)], refs[len(PARTS):]
     if near:
         states, (out, near_first, near_second, mixed), refs = refs[:4], refs[4:8], refs[8:]
         heads, rows, flat, held, near_peer, sems = refs
@@ -218,18 +232,18 @@
         copy.start()
     heads[...] = jnp.zeros_like(heads)
     total = jnp.zeros((LANES, QUARTER), F32)
-    for k, block in enumerate((*blocks[:-1], held)):
-        start = pl.multiple_of((place[0] + NY - k) % NY * TOK, TOK)
-        preact = jnp.zeros((TOK, HEAD), F32)
+    for block, (k, first, count) in zip((*blocks[:-1], held), PARTS):
+        start = pl.multiple_of((place[0] + NY - k) % NY * TOK + first, HALF)
+        preact = jnp.zeros((count, HEAD), F32)
         for s in range(NY):
-            preact = preact + partials[pl.ds(s * NY * TOK + start, TOK), :].astype(F32)
+            preact = preact + partials[pl.ds(s * NY * TOK + start, count), :].astype(F32)
         if block is held:
             copies[0].wait()
         cot = block[:, QUARTER:QUARTER + HEAD].astype(F32)
         sig = 1.0 / (1.0 + jnp.exp(-preact))
-        heads[:, :HEAD] = (cot * sig * (1.0 + preact * (1.0 - sig))).astype(BF16)
+        heads[:count, :HEAD] = (cot * sig * (1.0 + preact * (1.0 - sig))).astype(BF16)
         total = total + lax.dot_general(
-            heads[...], block[:, :QUARTER], (((0,), (0,)), ((), ())), preferred_element_type=F32
+            heads[:count], block[:, :QUARTER], (((0,), (0,)), ((), ())), preferred_element_type=F32
         )
     rows[...] = total.T
     flat[FLAT:, :] = jnp.zeros((WIRE - FLAT, LANES), F32)
@@ -246,7 +260,7 @@
     near = bool(states)
     return pl.pallas_call(
         functools.partial(grad_kernel, near),
-        in_specs=[SMEM] + [VMEM] * NY + [HBM] * (1 + len(states)),
+        in_specs=[SMEM] + [VMEM] * len(PARTS) + [HBM] * (1 + len(states)),
         out_specs=[VMEM] * (4 if near else 1),
         out_shape=[
             shape((NZ, WIRE, LANES), BF16),
@@ -258,7 +272,7 @@
             pltpu.VMEM((TOK, LANES), BF16),
             pltpu.VMEM((QUARTER, LANES), F32),
             pltpu.VMEM((WIRE, LANES), F32),
-            pltpu.VMEM((TOK, BLOCK), BF16),
+            pltpu.VMEM((PARTS[-1][2], BLOCK), BF16),
             *[pltpu.VMEM((WIRE, LANES), F32)] * near,
             DMA((1 + len(states),)),
         ],
@@ -373,8 +387,11 @@
     second_moment = second_moment.reshape(FLAT, LANES)
     own, wire = start(mass, params.reshape(FLAT, LANES))
     wire, scales, *picks = lax.optimization_barrier((wire, scales, *picks))
-    blocks = norm(place, tokens[0], cotangent[0].T)
-    blocks = [blocks[0]] + [y_shift(blocks[k], k) for k in range(1, NY)]
+    blocks = {}
+    for parts, rows_in in ((EARLY, HALF), (LATER, TOK)):
+        for part, block in zip(parts, norm(parts, rows_in, place, tokens[0], cotangent[0].T)):
+            blocks[part] = y_shift(block, part[0]) if part[0] else block
+    blocks = [blocks[part] for part in PARTS]
     for section in range(STEPS):
         if section == 0:
             wires = gather(wire, Z_GROUPS)

time: 196 us -> 190 us (0.969)
  blocking collectives: 146 us -> 137 us
  Pallas kernels: 19.3 us -> 23.3 us
  waiting for transfers between devices: 7.85 us -> 5.48 us
    all_to_all x2, blocking collectives: 65.2 us -> 56.7 us  [on_device(): terms = lax.all_to_all(terms, 'fsdp', 0, 0, axis_index_groups=Z_GROUPS)]
    pallas_call x3 -> x4, Pallas kernels: 8.71 us -> 12.3 us  [the longest x2 7.11 us: norm(): pl.pallas_call(functools.partial(norm_kernel, parts, rows_in), in_specs=[...]
    ppermute x2, starting transfers between devices: 8.16 us -> 5 us  [gossip(): lax.ppermute(array, 'rep', [(i, (i + distance) % count) for i in range(co...]
    ppermute x3 -> x4, starting transfers between devices: 11.6 us -> 14.4 us  [y_shift(): return lax.ppermute(array, 'fsdp', pairs)]
    ppermute x2, waiting for transfers between devices: 7.84 us -> 5.47 us  [gossip(): lax.ppermute(array, 'rep', [(i, (i + distance) % count) for i in range(co...]
  transfers between devices with their start and end apart: 5 -> 6, of which waited for: 1 -> 1; matrix products, arithmetic and copies ran while one was open for 0% -> 0% of each run, Pallas kernels for 0% -> 2%
where the time goes in v2:
time: 190 us; the launch traced here: 188 us
  blocking collectives  137 us (72%)
  Pallas kernels  23.3 us (12%)
  starting transfers between devices  19.4 us (10%)
  waiting for transfers between devices  5.48 us (3%)
  between operations  2.08 us (1%)
    all_gather x4, blocking collectives, gather(): lax.all_gather(array, 'fsdp', axis=0, tiled=True, axis_index_groups=groups)  80.5 us
    all_to_all x2, blocking collectives, on_device(): terms = lax.all_to_all(terms, 'fsdp', 0, 0, axis_index_groups=Z_GROUPS)  56.7 us
    ppermute x4, starting transfers between devices, y_shift(): return lax.ppermute(array, 'fsdp', pairs)  14.4 us
    pallas_call x2, Pallas kernels, norm(): pl.pallas_call(functools.partial(norm_kernel, parts, rows_in), in_specs=[...  7.11 us
    ppermute x2, waiting for transfers between devices, gossip(): lax.ppermute(array, 'rep', [(i, (i + distance) % count) for i in range(co...  5.47 us
    pallas_call x2, Pallas kernels, quarter_grad(): pl.pallas_call(functools.partial(grad_kernel, near), in_specs=[SMEM] + [V...  5.36 us
    pallas_call x2, Pallas kernels, partial_preact(): pl.pallas_call(preact_kernel, in_specs=[SMEM] + [VMEM] * len(PARTS) + [HB...  5.21 us
    ppermute x2, starting transfers between devices, gossip(): lax.ppermute(array, 'rep', [(i, (i + distance) % count) for i in range(co...  5 us
  transfers between devices with their start and end apart: 6, of which 1 were waited for; matrix products, arithmetic and copies ran while one was open for 0% of the time, Pallas kernels for 2%

profile of v2, /device:TPU:6, one launch (start us, length us, event | category | flops | bytes accessed | tf_op | source)
XLA Modules:
  0.0 187.8 jit_solution(9137337861010817673)
XLA Ops:
  0.6 0.0 copy-start
  0.7 4.4 %norm.2 = (bf16[128,1920]{1,0:T(8,128)(2,1)}, bf16[256,1920]{1,0:T(8,128)(2,1)}, bf16[256,1920]{1,0:T(8,128)(2,1)}, bf16[256,1920]{1,0:T(8,128)(2,1)S(1)}) custom-call(s32[1]{0:T(128)} %bitcast.3.place, bf16[256,7168]{1,0:T(8,128)(2,1)} %bitcast.14, bf16[112,256]{1,0:T(8,128)(2,1)} %bitcast.16), custom_call_target="tpu_custom_call" | custom-call | tf_op jit(solution)/shard_map/norm/pallas_call | solution.py:148
  5.1 3.5 %collective-permute-start.10 = (bf16[256,1920]{1,0:T(8,128)(2,1)}, bf16[256,1920]{1,0:T(8,128)(2,1)S(1)}, u32[]{:S(2)}, u32[]{:S(2)}) collective-permute-start(bf16[256,1920]{1,0:T(8,128)(2,1)} %get-tuple-element.85), channel_id=1, source_target_pairs={{0,4},{1,5},{2,6},{3,7},{4,8},{5,9},{6,10},{7,11},{8,12},{9,13},{1... | collective-permute-start | bytes 2949128 | tf_op jit(solution)/shard_map/ppermute | solution.py:57
  8.5 3.6 %collective-permute-start.13 = (bf16[256,1920]{1,0:T(8,128)(2,1)}, bf16[256,1920]{1,0:T(8,128)(2,1)}, u32[]{:S(2)}, u32[]{:S(2)}) collective-permute-start(bf16[256,1920]{1,0:T(8,128)(2,1)} %get-tuple-element.87), channel_id=1, source_target_pairs={{0,12},{1,13},{2,14},{3,15},{4,0},{5,1},{6,2},{7,3},{8,4},{9,5},{1... | collective-permute-start | bytes 2949128 | tf_op jit(solution)/shard_map/ppermute | solution.py:57
  12.1 2.7 %norm.3 = bf16[128,1920]{1,0:T(8,128)(2,1)} custom-call(s32[1]{0:T(128)} %bitcast.3.place, bf16[256,7168]{1,0:T(8,128)(2,1)} %bitcast.15, bf16[112,256]{1,0:T(8,128)(2,1)} %bitcast.17), custom_call_target="tpu_custom_call" | custom-call | tf_op jit(solution)/shard_map/norm/pallas_call | solution.py:148
  14.9 3.9 %collective-permute-start.11 = (bf16[128,1920]{1,0:T(8,128)(2,1)}, bf16[128,1920]{1,0:T(8,128)(2,1)S(1)}, u32[]{:S(2)}, u32[]{:S(2)}) collective-permute-start(bf16[128,1920]{1,0:T(8,128)(2,1)} %norm.3), channel_id=1, source_target_pairs={{0,8},{1,9},{2,10},{3,11},{4,12},{5,13},{6,14},{7,15},{8,0},{9,1},... | collective-permute-start | bytes 1474568 | tf_op jit(solution)/shard_map/ppermute | solution.py:57
  18.8 3.5 %collective-permute-start.12 = (bf16[128,1920]{1,0:T(8,128)(2,1)}, bf16[128,1920]{1,0:T(8,128)(2,1)S(1)}, u32[]{:S(2)}, u32[]{:S(2)}) collective-permute-start(bf16[128,1920]{1,0:T(8,128)(2,1)} %get-tuple-element.86), channel_id=1, source_target_pairs={{0,8},{1,9},{2,10},{3,11},{4,12},{5,13},{6,14},{7,15},{8,0},{9,1},... | collective-permute-start | bytes 1474568 | tf_op jit(solution)/shard_map/ppermute | solution.py:57
  23.6 0.1 pad_maximum_fusion
  23.6 0.1 reshape.60.scales
  23.7 0.0 copy-done
  23.7 0.7 start.1
  24.4 29.2 %all_gather.24.wires = bf16[1600,128]{1,0:T(8,128)(2,1)S(1)} all-gather(bf16[400,128]{1,0:T(8,128)(2,1)S(1)} %get-tuple-element.78), channel_id=1, replica_groups={{0,1,2,3},{4,5,6,7},{8,9,10,11},{12,13,14,15},{16,17,18,19},{20,21,22,2..., dimensions={0}, use_global_device_ids=true | all-gather | bytes 512000 | tf_op jit(solution)/shard_map/all_gather | solution.py:361
  53.6 7.4 %conditional.2 = (f32[400,128]{1,0:T(8,128)}) conditional(s32[]{:T(128)} %clamp.6, f32[400,128]{1,0:T(8,128)} %get-tuple-element.82.refs_2_, f32[400,128]{1,0:T(8,128)} %get-tuple-element.82.refs_2_, f32[400,128]{1,0:T(8,128)} %get-tuple-element.82.refs_2_, f32[400,128]{1,0:T(8,128)} %get-tuple-element.82.refs_2_, ...), branch_computations={%region_0.1_spmd, %region_1.2_spmd, %region_2.3_spmd, %region_3.4_... | conditional | bytes 819248 | solution.py:373
  53.6 1.9 %collective-permute-start = (f32[400,128]{1,0:T(8,128)}, f32[400,128]{1,0:T(8,128)}, u32[]{:S(2)}, u32[]{:S(2)}) collective-permute-start(f32[400,128]{1,0:T(8,128)} %param), channel_id=1, source_target_pairs={{0,16},{16,32},{32,48},{48,64},{64,80},{80,96},{96,112},{112,128},... | collective-permute-start | bytes 614408 | tf_op jit(solution)/shard_map/cond/branch_0_fun/ppermute | solution.py:62
  55.5 5.5 %collective-permute-done = f32[400,128]{1,0:T(8,128)} collective-permute-done((f32[400,128]{1,0:T(8,128)}, f32[400,128]{1,0:T(8,128)}, u32[]{:S(2)}, u32[]{:S(2)}) %collective-permute-start) | collective-permute-done | bytes 204832 | tf_op jit(solution)/shard_map/cond/branch_0_fun/ppermute | solution.py:62
  61.0 0.0 collective-permute-done.11.refs_2_
  61.0 0.0 collective-permute-done.12.refs_3_
  61.0 0.0 collective-permute-done.10.refs_1_
  61.0 0.0 collective-permute-done.13.refs_4_
  61.0 2.6 %partial_preact.2 = bf16[1024,112]{1,0:T(8,128)(2,1)S(1)} custom-call(s32[1]{0:T(128)} %bitcast.3.place, bf16[1600,128]{1,0:T(8,128)(2,1)S(1)} %all_gather.24.wires, bf16[256,1920]{1,0:T(8,128)(2,1)S(1)} %get-tuple-element.84.refs_0_, bf16[256,1920]{1,0:T(8,128)(2,1)S(1)} %collective-permute-done.10.refs_1_, ...), custom_call_target="tpu_custom_call" | custom-call | tf_op jit(solution)/shard_map/partial_preact/pallas_call | solution.py:202
  63.6 15.0 %all_gather.25.partials = bf16[4096,112]{1,0:T(8,128)(2,1)S(1)} all-gather(bf16[1024,112]{1,0:T(8,128)(2,1)S(1)} %partial_preact.2), channel_id=1, replica_groups={{0,4,8,12},{1,5,9,13},{2,6,10,14},{3,7,11,15},{16,20,24,28},{17,21,25,2..., dimensions={0}, use_global_device_ids=true | all-gather | bytes 1146880 | tf_op jit(solution)/shard_map/all_gather | solution.py:361
  78.6 2.6 %quarter_grad.2 = bf16[4,400,128]{2,1,0:T(8,128)(2,1)S(1)} custom-call(s32[1]{0:T(128)} %bitcast.3.place, bf16[4096,112]{1,0:T(8,128)(2,1)S(1)} %all_gather.25.partials, bf16[256,1920]{1,0:T(8,128)(2,1)S(1)} %get-tuple-element.84.refs_0_, bf16[256,1920]{1,0:T(8,128)(2,1)S(1)} %collective-permute-done.10.refs_1_, ...), custom_call_target="tpu_custom_call" | custom-call | tf_op jit(solution)/shard_map/quarter_grad/pallas_call | solution.py:261
  81.2 30.6 %all_to_all.10.terms = bf16[4,400,128]{2,1,0:T(8,128)(2,1)S(1)} all-to-all(bf16[4,400,128]{2,1,0:T(8,128)(2,1)S(1)} %quarter_grad.2), channel_id=1, replica_groups={{0,1,2,3},{4,5,6,7},{8,9,10,11},{12,13,14,15},{16,17,18,19},{20,21,22,2..., dimensions={0} | all-to-all | bytes 819200 | tf_op jit(solution)/shard_map/all_to_all | solution.py:406
  111.8 3.4 %between.1 = (f32[392,128]{1,0:T(8,128)}, f32[392,128]{1,0:T(8,128)}, f32[400,128]{1,0:T(8,128)}, bf16[400,128]{1,0:T(8,128)(2,1)S(1)}) custom-call(f32[4]{0:T(128)S(1)} %reshape.60.scales, bf16[4,400,128]{2,1,0:T(8,128)(2,1)S(1)} %all_to_all.10.terms, f32[392,128]{1,0:T(8,128)} %bitcast.18, f32[392,128]{1,0:T(8,128)} %bitcast.19, ...), custom_call_target="tpu_custom_call" | custom-call | tf_op jit(solution)/shard_map/between/pallas_call | solution.py:324
  115.2 25.4 %conditional.3 = (f32[400,128]{1,0:T(8,128)}, bf16[1600,128]{1,0:T(8,128)(2,1)S(1)}) conditional(s32[]{:T(128)} %clamp.7, (f32[400,128]{1,0:T(8,128)}, bf16[400,128]{1,0:T(8,128)(2,1)S(1)}) %tuple.53, (f32[400,128]{1,0:T(8,128)}, bf16[400,128]{1,0:T(8,128)(2,1)S(1)}) %tuple.53, (f32[400,128]{1,0:T(8,128)}, ...), branch_computations={%region_5.6_spmd, %region_6.7_spmd, %region_7.8_spmd, %region_8.9_... | conditional | bytes 1331256 | solution.py:373
  115.2 3.1 %collective-permute-start.6 = (f32[400,128]{1,0:T(8,128)}, f32[400,128]{1,0:T(8,128)}, u32[]{:S(2)}, u32[]{:S(2)}) collective-permute-start(f32[400,128]{1,0:T(8,128)} %get-tuple-element.33), channel_id=1, source_target_pairs={{0,32},{16,48},{32,64},{48,80},{64,96},{80,112},{96,128},{112,144}... | collective-permute-start | bytes 614408 | tf_op jit(solution)/shard_map/cond/branch_1_fun/ppermute | solution.py:62
  118.3 22.3 %all_gather.17 = bf16[1600,128]{1,0:T(8,128)(2,1)S(1)} all-gather(bf16[400,128]{1,0:T(8,128)(2,1)S(1)} %get-tuple-element.34), channel_id=1, replica_groups={{0,1,2,3},{4,5,6,7},{8,9,10,11},{12,13,14,15},{16,17,18,19},{20,21,22,2..., dimensions={0}, use_global_device_ids=true | all-gather | bytes 512000 | tf_op jit(solution)/shard_map/cond/branch_1_fun/all_gather | solution.py:361
  140.6 0.0 collective-permute-done.6
  140.6 2.6 %partial_preact.3 = bf16[1024,112]{1,0:T(8,128)(2,1)S(1)} custom-call(s32[1]{0:T(128)} %bitcast.3.place, bf16[1600,128]{1,0:T(8,128)(2,1)S(1)} %get-tuple-element.94.wires, bf16[256,1920]{1,0:T(8,128)(2,1)S(1)} %get-tuple-element.84.refs_0_, bf16[256,1920]{1,0:T(8,128)(2,1)S(1)} %collective-permute-done.10.refs_1_, ...), custom_call_target="tpu_custom_call" | custom-call | tf_op jit(solution)/shard_map/partial_preact/pallas_call | solution.py:202
  143.2 14.0 %all_gather.26.partials = bf16[4096,112]{1,0:T(8,128)(2,1)S(1)} all-gather(bf16[1024,112]{1,0:T(8,128)(2,1)S(1)} %partial_preact.3), channel_id=1, replica_groups={{0,4,8,12},{1,5,9,13},{2,6,10,14},{3,7,11,15},{16,20,24,28},{17,21,25,2..., dimensions={0}, use_global_device_ids=true | all-gather | bytes 1146880 | tf_op jit(solution)/shard_map/all_gather | solution.py:361
  157.2 2.8 %quarter_grad.3 = (bf16[4,400,128]{2,1,0:T(8,128)(2,1)S(1)}, f32[392,128]{1,0:T(8,128)S(1)}, f32[392,128]{1,0:T(8,128)S(1)}, f32[400,128]{1,0:T(8,128)S(1)}) custom-call(s32[1]{0:T(128)} %bitcast.3.place, bf16[4096,112]{1,0:T(8,128)(2,1)S(1)} %all_gather.26.partials, bf16[256,1920]{1,0:T(8,128)(2,1)S(1)} %get-tuple-element.84.refs_0_, ...), custom_call_target="tpu_custom_call" | custom-call | tf_op jit(solution)/shard_map/quarter_grad/pallas_call | solution.py:261
  160.0 26.2 %all_to_all.11.terms = bf16[4,400,128]{2,1,0:T(8,128)(2,1)S(1)} all-to-all(bf16[4,400,128]{2,1,0:T(8,128)(2,1)S(1)} %get-tuple-element.98), channel_id=1, replica_groups={{0,1,2,3},{4,5,6,7},{8,9,10,11},{12,13,14,15},{16,17,18,19},{20,21,22,2..., dimensions={0} | all-to-all | bytes 819200 | tf_op jit(solution)/shard_map/all_to_all | solution.py:406
  186.2 1.5 last.1
  (1 shorter events, 0.0 us)
Async XLA Ops:
  0.6 23.1 %copy-start = (f32[1,50176]{1,0:T(1,128)S(1)}, f32[1,50176]{1,0:T(1,128)}, u32[]{:S(2)}) copy-start(f32[1,50176]{1,0:T(1,128)} %param.19) | copy-start | bytes 602116
  5.1 55.9 %collective-permute-start.10 = (bf16[256,1920]{1,0:T(8,128)(2,1)}, bf16[256,1920]{1,0:T(8,128)(2,1)S(1)}, u32[]{:S(2)}, u32[]{:S(2)}) collective-permute-start(bf16[256,1920]{1,0:T(8,128)(2,1)} %get-tuple-element.85), channel_id=1, source_target_pairs={{0,4},{1,5},{2,6},{3,7},{4,8},{5,9},{6,10},{7,11},{8,12},{9,13},{1... | collective-permute-start | bytes 2949128 | tf_op jit(solution)/shard_map/ppermute | solution.py:57
  8.5 52.4 %collective-permute-start.13 = (bf16[256,1920]{1,0:T(8,128)(2,1)}, bf16[256,1920]{1,0:T(8,128)(2,1)}, u32[]{:S(2)}, u32[]{:S(2)}) collective-permute-start(bf16[256,1920]{1,0:T(8,128)(2,1)} %get-tuple-element.87), channel_id=1, source_target_pairs={{0,12},{1,13},{2,14},{3,15},{4,0},{5,1},{6,2},{7,3},{8,4},{9,5},{1... | collective-permute-start | bytes 2949128 | tf_op jit(solution)/shard_map/ppermute | solution.py:57
  14.9 46.1 %collective-permute-start.11 = (bf16[128,1920]{1,0:T(8,128)(2,1)}, bf16[128,1920]{1,0:T(8,128)(2,1)S(1)}, u32[]{:S(2)}, u32[]{:S(2)}) collective-permute-start(bf16[128,1920]{1,0:T(8,128)(2,1)} %norm.3), channel_id=1, source_target_pairs={{0,8},{1,9},{2,10},{3,11},{4,12},{5,13},{6,14},{7,15},{8,0},{9,1},... | collective-permute-start | bytes 1474568 | tf_op jit(solution)/shard_map/ppermute | solution.py:57
  18.8 42.2 %collective-permute-start.12 = (bf16[128,1920]{1,0:T(8,128)(2,1)}, bf16[128,1920]{1,0:T(8,128)(2,1)S(1)}, u32[]{:S(2)}, u32[]{:S(2)}) collective-permute-start(bf16[128,1920]{1,0:T(8,128)(2,1)} %get-tuple-element.86), channel_id=1, source_target_pairs={{0,8},{1,9},{2,10},{3,11},{4,12},{5,13},{6,14},{7,15},{8,0},{9,1},... | collective-permute-start | bytes 1474568 | tf_op jit(solution)/shard_map/ppermute | solution.py:57
  53.6 7.4 %collective-permute-start = (f32[400,128]{1,0:T(8,128)}, f32[400,128]{1,0:T(8,128)}, u32[]{:S(2)}, u32[]{:S(2)}) collective-permute-start(f32[400,128]{1,0:T(8,128)} %param), channel_id=1, source_target_pairs={{0,16},{16,32},{32,48},{48,64},{64,80},{80,96},{96,112},{112,128},... | collective-permute-start | bytes 614408 | tf_op jit(solution)/shard_map/cond/branch_0_fun/ppermute | solution.py:62
  115.2 25.4 %collective-permute-start.6 = (f32[400,128]{1,0:T(8,128)}, f32[400,128]{1,0:T(8,128)}, u32[]{:S(2)}, u32[]{:S(2)}) collective-permute-start(f32[400,128]{1,0:T(8,128)} %get-tuple-element.33), channel_id=1, source_target_pairs={{0,32},{16,48},{32,64},{48,80},{64,96},{80,112},{96,128},{112,144}... | collective-permute-start | bytes 614408 | tf_op jit(solution)/shard_map/cond/branch_1_fun/ppermute | solution.py:62

commit v3 on v1

--- a/solution.py
+++ b/solution.py
@@ -22,6 +22,8 @@
 BLOCK = QUARTER + LANES
 CHUNKS = 4
 CHUNK = TOK // CHUNKS
+HALF = TOK // 2
+PARTS = ((0, 0, TOK), (1, 0, TOK), (2, 0, HALF), (2, HALF, HALF), (3, 0, TOK))
 
 BETA_ONE = 0.9
 BETA_TWO = 0.95
@@ -87,8 +89,18 @@
         flat[pl.ds(i, GROUPS, stride=7), :] = jnp.where(lane < HEAD - 16 * i, first, second)
 
 
+def scaled(values, center, scale, out, width=QUARTER):
+    for c in range(width // LANES):
+        lanes = slice(c * LANES, (c + 1) * LANES)
+        out[:, lanes] = ((values[:, lanes].astype(F32) - center) * scale).astype(BF16)
+
+
+def padded_cotangent(cot):
+    return jnp.concatenate([cot[...], jnp.zeros((LANES - HEAD, TOK), BF16)], axis=0).T
+
+
 def norm_kernel(place, tokens, cotangent, *refs):
-    (own, *far), (values, cot, near, sems, out_sems) = refs[:NY], refs[NY:]
+    outs, (centers, scales, values, cot, nears, sems, out_sems) = refs[:2], refs[2:]
     chunks = [pl.ds(i * CHUNK, CHUNK) for i in range(CHUNKS)]
     copies = [
         pltpu.make_async_copy(tokens.at[rows], values.at[rows], sems.at[i])
@@ -97,11 +109,10 @@
     copies.append(pltpu.make_async_copy(cotangent, cot, sems.at[CHUNKS]))
     for copy in (copies[-1], *copies[:-1]):
         copy.start()
-    outs = [own, *(near.at[k] for k in range(NY - 1))]
     copies[-1].wait()
-    padded = jnp.concatenate([cot[...], jnp.zeros((LANES - HEAD, TOK), BF16)], axis=0).T
-    for out in outs:
-        out[:, QUARTER:] = padded
+    padded = padded_cotangent(cot)
+    for n in range(2):
+        nears[n, :, QUARTER:] = padded
     sent = []
     for i, rows in enumerate(chunks):
         copies[i].wait()
@@ -116,19 +127,18 @@
             totals[c % 2] += apart * apart
         spread = jnp.sum(sum(totals), axis=-1, keepdims=True) * (1.0 / D)
         scale = jnp.broadcast_to(lax.rsqrt(spread + 1e-05), (CHUNK, LANES))
-        for k in (*range(1, NY), 0):
+        centers[rows] = center
+        scales[rows] = scale
+        for n, k in enumerate((1, 3)):
             start = (place[0] + k) % NY * QUARTER
             for c in range(QUARTER // LANES):
                 lanes = pl.ds(pl.multiple_of(start + c * LANES, LANES), LANES)
                 part = (values[rows, lanes].astype(F32) - center) * scale
-                outs[k][rows, c * LANES:(c + 1) * LANES] = part.astype(BF16)
-            if k:
-                sent.append(
-                    pltpu.make_async_copy(
-                        near.at[k - 1, rows], far[k - 1].at[rows], out_sems.at[i, k - 1]
-                    )
-                )
-                sent[-1].start()
+                nears[n, rows, c * LANES:(c + 1) * LANES] = part.astype(BF16)
+            sent.append(
+                pltpu.make_async_copy(nears.at[n, rows], outs[n].at[rows], out_sems.at[n, i])
+            )
+            sent[-1].start()
     for copy in sent:
         copy.wait()
 
@@ -137,18 +147,67 @@
     return pl.pallas_call(
         norm_kernel,
         in_specs=[SMEM, HBM, HBM],
-        out_specs=[VMEM] + [HBM] * (NY - 1),
-        out_shape=[shape((TOK, BLOCK), BF16)] + [pltpu.HBM((TOK, BLOCK), BF16)] * (NY - 1),
+        out_specs=[HBM] * 2 + [VMEM] * 2,
+        out_shape=[pltpu.HBM((TOK, BLOCK), BF16)] * 2 + [shape((TOK, LANES), F32)] * 2,
         scratch_shapes=[
             pltpu.VMEM((TOK, D), BF16),
             pltpu.VMEM((HEAD, TOK), BF16),
-            pltpu.VMEM((NY - 1, TOK, BLOCK), BF16),
+            pltpu.VMEM((2, TOK, BLOCK), BF16),
             DMA((CHUNKS + 1,)),
-            DMA((CHUNKS, NY - 1)),
+            DMA((2, CHUNKS)),
         ],
         compiler_params=PARAMS,
         name="norm",
     )(place, in_hbm(tokens), in_hbm(cotangent))
+
+
+def later_norm_kernel(place, tokens, cotangent, centers, scales, *refs):
+    (own, *outs), (values, cot, nears, sems, out_sems) = refs[:3], refs[3:]
+    halves = [pl.ds(h * HALF, HALF) for h in range(2)]
+    copies = [pltpu.make_async_copy(cotangent, cot, sems.at[4])]
+    for n, k in enumerate((2, 0)):
+        start = pl.multiple_of((place[0] + k) % NY * QUARTER, LANES)
+        for h, rows in enumerate(halves):
+            copies.append(
+                pltpu.make_async_copy(
+                    tokens.at[rows, pl.ds(start, QUARTER)], values.at[n, rows], sems.at[2 * n + h]
+                )
+            )
+    for copy in copies:
+        copy.start()
+    copies[0].wait()
+    padded = padded_cotangent(cot)
+    own[:, QUARTER:] = padded
+    sent = []
+    for h, rows in enumerate(halves):
+        nears[h, :, QUARTER:] = padded[h * HALF:(h + 1) * HALF]
+        copies[1 + h].wait()
+        scaled(values.at[0, rows], centers[rows], scales[rows], nears.at[h])
+        sent.append(pltpu.make_async_copy(nears.at[h], outs[h], out_sems.at[h]))
+        sent[-1].start()
+    for h, rows in enumerate(halves):
+        copies[3 + h].wait()
+        scaled(values.at[1, rows], centers[rows], scales[rows], own.at[rows])
+    for copy in sent:
+        copy.wait()
+
+
+def later_norm(place, tokens, cotangent, centers, scales):
+    return pl.pallas_call(
+        later_norm_kernel,
+        in_specs=[SMEM, HBM, HBM, VMEM, VMEM],
+        out_specs=[VMEM] + [HBM] * 2,
+        out_shape=[shape((TOK, BLOCK), BF16)] + [pltpu.HBM((HALF, BLOCK), BF16)] * 2,
+        scratch_shapes=[
+            pltpu.VMEM((2, TOK, QUARTER), BF16),
+            pltpu.VMEM((HEAD, TOK), BF16),
+            pltpu.VMEM((2, HALF, BLOCK), BF16),
+            DMA((5,)),
+            DMA((2,)),
+        ],
+        compiler_params=PARAMS,
+        name="later_norm",
+    )(place, in_hbm(tokens), in_hbm(cotangent), centers, scales)
 
 
 def start_kernel(mass, params, own, wire):
@@ -169,32 +228,32 @@
 
 
 def preact_kernel(place, wires, *refs):
-    blocks, (out, flat, rows, weights, held, sem) = refs[:NY], refs[NY:]
+    blocks, (out, flat, rows, weights, held, sem) = refs[:len(PARTS)], refs[len(PARTS):]
     fetch = pltpu.make_async_copy(blocks[-1], held, sem)
     fetch.start()
     flat[...] = wires[...].astype(F32)
     for s in range(NZ):
         flat_to_rows(flat, s * WIRE, rows)
-        weights[pl.ds(s * SHARD_ROWS, SHARD_ROWS), :] = rows[...].astype(BF16)
-    for k, block in enumerate((*blocks[:-1], held)):
+        weights[pl.ds(s * SHARD_ROWS, SHARD_ROWS), :] = rows[:SHARD_ROWS, :].astype(BF16)
+    for block, (k, first, count) in zip((*blocks[:-1], held), PARTS):
         if block is held:
             fetch.wait()
         product = jnp.dot(block[:, :QUARTER], weights[...], preferred_element_type=F32)
-        start = pl.multiple_of((place[0] + NY - k) % NY * TOK, TOK)
-        out[pl.ds(start, TOK), :] = product[:, :HEAD].astype(BF16)
+        start = pl.multiple_of((place[0] + NY - k) % NY * TOK + first, HALF)
+        out[pl.ds(start, count), :] = product[:, :HEAD].astype(BF16)
 
 
 def partial_preact(place, wires, blocks):
     return pl.pallas_call(
         preact_kernel,
-        in_specs=[SMEM] + [VMEM] * NY + [HBM],
+        in_specs=[SMEM] + [VMEM] * len(PARTS) + [HBM],
         out_specs=VMEM,
         out_shape=shape((NY * TOK, HEAD), BF16),
         scratch_shapes=[
             pltpu.VMEM((NZ * WIRE, LANES), F32),
-            pltpu.VMEM((SHARD_ROWS, LANES), F32),
+            pltpu.VMEM((SHARD_ROWS + 8, LANES), F32),
             pltpu.VMEM((QUARTER, LANES), BF16),
-            pltpu.VMEM((TOK, BLOCK), BF16),
+            pltpu.VMEM((PARTS[-1][2], BLOCK), BF16),
             DMA,
         ],
         compiler_params=PARAMS,
@@ -203,7 +262,7 @@
 
 
 def grad_kernel(near, place, partials, *refs):
-    blocks, refs = refs[:NY], refs[NY:]
+    blocks, refs = refs[:len(PARTS)], refs[len(PARTS):]
     if near:
         states, (out, near_first, near_second, mixed), refs = refs[:4], refs[4:8], refs[8:]
         heads, rows, flat, held, near_peer, sems = refs
@@ -218,20 +277,20 @@
         copy.start()
     heads[...] = jnp.zeros_like(heads)
     total = jnp.zeros((LANES, QUARTER), F32)
-    for k, block in enumerate((*blocks[:-1], held)):
-        start = pl.multiple_of((place[0] + NY - k) % NY * TOK, TOK)
-        preact = jnp.zeros((TOK, HEAD), F32)
+    for block, (k, first, count) in zip((*blocks[:-1], held), PARTS):
+        start = pl.multiple_of((place[0] + NY - k) % NY * TOK + first, HALF)
+        preact = jnp.zeros((count, HEAD), F32)
         for s in range(NY):
-            preact = preact + partials[pl.ds(s * NY * TOK + start, TOK), :].astype(F32)
+            preact = preact + partials[pl.ds(s * NY * TOK + start, count), :].astype(F32)
         if block is held:
             copies[0].wait()
         cot = block[:, QUARTER:QUARTER + HEAD].astype(F32)
         sig = 1.0 / (1.0 + jnp.exp(-preact))
-        heads[:, :HEAD] = (cot * sig * (1.0 + preact * (1.0 - sig))).astype(BF16)
+        heads[:count, :HEAD] = (cot * sig * (1.0 + preact * (1.0 - sig))).astype(BF16)
         total = total + lax.dot_general(
-            heads[...], block[:, :QUARTER], (((0,), (0,)), ((), ())), preferred_element_type=F32
+            heads[:count], block[:, :QUARTER], (((0,), (0,)), ((), ())), preferred_element_type=F32
         )
-    rows[...] = total.T
+    rows[:QUARTER, :] = total.T
     flat[FLAT:, :] = jnp.zeros((WIRE - FLAT, LANES), F32)
     for s in range(NZ):
         rows_to_flat(rows, s * SHARD_ROWS, flat)
@@ -246,7 +305,7 @@
     near = bool(states)
     return pl.pallas_call(
         functools.partial(grad_kernel, near),
-        in_specs=[SMEM] + [VMEM] * NY + [HBM] * (1 + len(states)),
+        in_specs=[SMEM] + [VMEM] * len(PARTS) + [HBM] * (1 + len(states)),
         out_specs=[VMEM] * (4 if near else 1),
         out_shape=[
             shape((NZ, WIRE, LANES), BF16),
@@ -256,9 +315,9 @@
         ][:4 if near else 1],
         scratch_shapes=[
             pltpu.VMEM((TOK, LANES), BF16),
-            pltpu.VMEM((QUARTER, LANES), F32),
+            pltpu.VMEM((QUARTER + 8, LANES), F32),
             pltpu.VMEM((WIRE, LANES), F32),
-            pltpu.VMEM((TOK, BLOCK), BF16),
+            pltpu.VMEM((PARTS[-1][2], BLOCK), BF16),
             *[pltpu.VMEM((WIRE, LANES), F32)] * near,
             DMA((1 + len(states),)),
         ],
@@ -267,11 +326,14 @@
     )(place, partials, *blocks[:-1], in_hbm(blocks[-1]), *map(in_hbm, states))
 
 
-def adam(section, scales, terms, first_moment, second_moment, mixed):
+def summed(terms):
     grads = terms[0].astype(F32)
     for s in range(1, NZ):
         grads = grads + terms[s].astype(F32)
-    grads = grads[:FLAT, :]
+    return grads[:FLAT, :]
+
+
+def adam(section, scales, grads, first_moment, second_moment, mixed):
     first = BETA_ONE * first_moment[...] + (1.0 - BETA_ONE) * grads
     second = BETA_TWO * second_moment[...] + (1.0 - BETA_TWO) * grads * grads
     update = first / scales[2 * section] / (jnp.sqrt(second / scales[2 * section + 1]) + ADAM_EPS)
@@ -290,10 +352,11 @@
     ]
     for copy in copies[:4]:
         copy.start()
+    grads = summed(terms)
     for copy in copies[:4]:
         copy.wait()
     own[...] = 0.5 * (own[...] + peer[...])
-    first, second, params, mass = adam(0, scales, terms, first_moment, second_moment, own)
+    first, second, params, mass = adam(0, scales, grads, first_moment, second_moment, own)
     new_first[...] = first
     new_second[...] = second
     for copy in copies[4:]:
@@ -325,7 +388,7 @@
 
 def last_kernel(scales, terms, first_moment, second_moment, mixed, *outs):
     new_params, new_first, new_second, new_mass = outs
-    first, second, params, mass = adam(1, scales, terms, first_moment, second_moment, mixed)
+    first, second, params, mass = adam(1, scales, summed(terms), first_moment, second_moment, mixed)
     new_first[...] = first
     new_second[...] = second
     new_params[...] = params
@@ -373,8 +436,10 @@
     second_moment = second_moment.reshape(FLAT, LANES)
     own, wire = start(mass, params.reshape(FLAT, LANES))
     wire, scales, *picks = lax.optimization_barrier((wire, scales, *picks))
-    blocks = norm(place, tokens[0], cotangent[0].T)
-    blocks = [blocks[0]] + [y_shift(blocks[k], k) for k in range(1, NY)]
+    one, three, *stats = norm(place, tokens[0], cotangent[0].T)
+    own_block, *two = later_norm(place, tokens[0], cotangent[0].T, *stats)
+    blocks = [own_block, one, *two, three]
+    blocks = [y_shift(block, part[0]) if part[0] else block for block, part in zip(blocks, PARTS)]
     for section in range(STEPS):
         if section == 0:
             wires = gather(wire, Z_GROUPS)

time: 196 us -> 192 us (0.980)
  the two profiles are of different devices: /device:TPU:6 before, /device:TPU:32 now
where the time goes in v3:
time: 192 us; the launch traced here: 189 us
  blocking collectives  139 us (72%)
  Pallas kernels  22.4 us (12%)
  starting transfers between devices  20.3 us (11%)
  waiting for transfers between devices  5.07 us (3%)
  between operations  2.08 us (1%)
    all_gather x4, blocking collectives, gather(): lax.all_gather(array, 'fsdp', axis=0, tiled=True, axis_index_groups=groups)  83.5 us
    all_to_all x2, blocking collectives, on_device(): terms = lax.all_to_all(terms, 'fsdp', 0, 0, axis_index_groups=Z_GROUPS)  55.2 us
    ppermute x4, starting transfers between devices, y_shift(): return lax.ppermute(array, 'fsdp', pairs)  14.4 us
    ppermute x2, starting transfers between devices, gossip(): lax.ppermute(array, 'rep', [(i, (i + distance) % count) for i in range(co...  5.94 us
    pallas_call x2, Pallas kernels, quarter_grad(): pl.pallas_call(functools.partial(grad_kernel, near), in_specs=[SMEM] + [V...  5.36 us
    pallas_call x2, Pallas kernels, partial_preact(): pl.pallas_call(preact_kernel, in_specs=[SMEM] + [VMEM] * len(PARTS) + [HB...  5.21 us
    ppermute x2, waiting for transfers between devices, gossip(): lax.ppermute(array, 'rep', [(i, (i + distance) % count) for i in range(co...  5.06 us
    pallas_call x1, Pallas kernels, norm(): pl.pallas_call(norm_kernel, in_specs=[SMEM, HBM, HBM], out_specs=[HBM] *...  4.01 us
  transfers between devices with their start and end apart: 6, of which 1 were waited for; matrix products, arithmetic and copies ran while one was open for 0% of the time, Pallas kernels for 2%

profile of v3, /device:TPU:32, one launch (start us, length us, event | category | flops | bytes accessed | tf_op | source)
XLA Modules:
  0.0 188.8 jit_solution(15778476156848756789)
XLA Ops:
  0.6 0.0 copy-start
  0.7 4.0 %norm.1 = (bf16[256,1920]{1,0:T(8,128)(2,1)}, bf16[256,1920]{1,0:T(8,128)(2,1)}, f32[256,128]{1,0:T(8,128)S(1)}, f32[256,128]{1,0:T(8,128)S(1)}) custom-call(s32[1]{0:T(128)} %bitcast.3.place, bf16[256,7168]{1,0:T(8,128)(2,1)} %bitcast.14, bf16[112,256]{1,0:T(8,128)(2,1)} %bitcast.16), custom_call_target="tpu_custom_call" | custom-call | tf_op jit(solution)/shard_map/norm/pallas_call | solution.py:147
  4.7 3.5 %collective-permute-start.10 = (bf16[256,1920]{1,0:T(8,128)(2,1)}, bf16[256,1920]{1,0:T(8,128)(2,1)S(1)}, u32[]{:S(2)}, u32[]{:S(2)}) collective-permute-start(bf16[256,1920]{1,0:T(8,128)(2,1)} %get-tuple-element.90), channel_id=1, source_target_pairs={{0,4},{1,5},{2,6},{3,7},{4,8},{5,9},{6,10},{7,11},{8,12},{9,13},{1... | collective-permute-start | bytes 2949128 | tf_op jit(solution)/shard_map/ppermute | solution.py:55
  8.2 3.6 %collective-permute-start.13 = (bf16[256,1920]{1,0:T(8,128)(2,1)}, bf16[256,1920]{1,0:T(8,128)(2,1)}, u32[]{:S(2)}, u32[]{:S(2)}) collective-permute-start(bf16[256,1920]{1,0:T(8,128)(2,1)} %get-tuple-element.93), channel_id=1, source_target_pairs={{0,12},{1,13},{2,14},{3,15},{4,0},{5,1},{6,2},{7,3},{8,4},{9,5},{1... | collective-permute-start | bytes 2949128 | tf_op jit(solution)/shard_map/ppermute | solution.py:55
  11.7 2.2 %later_norm.1 = (bf16[256,1920]{1,0:T(8,128)(2,1)S(1)}, bf16[128,1920]{1,0:T(8,128)(2,1)}, bf16[128,1920]{1,0:T(8,128)(2,1)}) custom-call(s32[1]{0:T(128)} %bitcast.3.place, bf16[256,7168]{1,0:T(8,128)(2,1)} %bitcast.15, bf16[112,256]{1,0:T(8,128)(2,1)} %bitcast.17, f32[256,128]{1,0:T(8,128)S(1)} %get-tuple-element.87.centers, ...), custom_call_target="tpu_custom_call" | custom-call | tf_op jit(solution)/shard_map/later_norm/pallas_call | solution.py:196
  13.9 3.9 %collective-permute-start.11 = (bf16[128,1920]{1,0:T(8,128)(2,1)}, bf16[128,1920]{1,0:T(8,128)(2,1)S(1)}, u32[]{:S(2)}, u32[]{:S(2)}) collective-permute-start(bf16[128,1920]{1,0:T(8,128)(2,1)} %get-tuple-element.91), channel_id=1, source_target_pairs={{0,8},{1,9},{2,10},{3,11},{4,12},{5,13},{6,14},{7,15},{8,0},{9,1},... | collective-permute-start | bytes 1474568 | tf_op jit(solution)/shard_map/ppermute | solution.py:55
  17.8 3.5 %collective-permute-start.12 = (bf16[128,1920]{1,0:T(8,128)(2,1)}, bf16[128,1920]{1,0:T(8,128)(2,1)S(1)}, u32[]{:S(2)}, u32[]{:S(2)}) collective-permute-start(bf16[128,1920]{1,0:T(8,128)(2,1)} %get-tuple-element.92), channel_id=1, source_target_pairs={{0,8},{1,9},{2,10},{3,11},{4,12},{5,13},{6,14},{7,15},{8,0},{9,1},... | collective-permute-start | bytes 1474568 | tf_op jit(solution)/shard_map/ppermute | solution.py:55
  22.6 0.1 pad_maximum_fusion
  22.7 0.1 reshape.60.scales
  22.8 0.0 copy-done
  22.8 0.7 start.1
  23.5 28.5 %all_gather.24.wires = bf16[1600,128]{1,0:T(8,128)(2,1)S(1)} all-gather(bf16[400,128]{1,0:T(8,128)(2,1)S(1)} %get-tuple-element.81), channel_id=1, replica_groups={{0,1,2,3},{4,5,6,7},{8,9,10,11},{12,13,14,15},{16,17,18,19},{20,21,22,2..., dimensions={0}, use_global_device_ids=true | all-gather | bytes 512000 | tf_op jit(solution)/shard_map/all_gather | solution.py:410
  52.0 8.0 %conditional.2 = (f32[400,128]{1,0:T(8,128)}) conditional(s32[]{:T(128)} %clamp.6, f32[400,128]{1,0:T(8,128)} %get-tuple-element.85.refs_2_, f32[400,128]{1,0:T(8,128)} %get-tuple-element.85.refs_2_, f32[400,128]{1,0:T(8,128)} %get-tuple-element.85.refs_2_, f32[400,128]{1,0:T(8,128)} %get-tuple-element.85.refs_2_, ...), branch_computations={%region_0.1_spmd, %region_1.2_spmd, %region_2.3_spmd, %region_3.4_... | conditional | bytes 819248 | solution.py:422
  52.0 2.9 %collective-permute-start.3 = (f32[400,128]{1,0:T(8,128)}, f32[400,128]{1,0:T(8,128)}, u32[]{:S(2)}, u32[]{:S(2)}) collective-permute-start(f32[400,128]{1,0:T(8,128)} %param.3), channel_id=1, source_target_pairs={{0,128},{16,144},{32,160},{48,176},{64,192},{80,208},{96,224},{112... | collective-permute-start | bytes 614408 | tf_op jit(solution)/shard_map/cond/branch_3_fun/ppermute | solution.py:60
  54.9 5.1 %collective-permute-done.3 = f32[400,128]{1,0:T(8,128)} collective-permute-done((f32[400,128]{1,0:T(8,128)}, f32[400,128]{1,0:T(8,128)}, u32[]{:S(2)}, u32[]{:S(2)}) %collective-permute-start.3) | collective-permute-done | bytes 204832 | tf_op jit(solution)/shard_map/cond/branch_3_fun/ppermute | solution.py:60
  60.0 0.0 collective-permute-done.11.refs_2_
  60.0 0.0 collective-permute-done.12.refs_3_
  60.0 0.0 collective-permute-done.10.refs_1_
  60.0 0.0 collective-permute-done.13.refs_4_
  60.0 2.6 %partial_preact.2 = bf16[1024,112]{1,0:T(8,128)(2,1)S(1)} custom-call(s32[1]{0:T(128)} %bitcast.3.place, bf16[1600,128]{1,0:T(8,128)(2,1)S(1)} %all_gather.24.wires, bf16[256,1920]{1,0:T(8,128)(2,1)S(1)} %get-tuple-element.89.refs_0_, bf16[256,1920]{1,0:T(8,128)(2,1)S(1)} %collective-permute-done.10.refs_1_, ...), custom_call_target="tpu_custom_call" | custom-call | tf_op jit(solution)/shard_map/partial_preact/pallas_call | solution.py:247
  62.6 14.5 %all_gather.25.partials = bf16[4096,112]{1,0:T(8,128)(2,1)S(1)} all-gather(bf16[1024,112]{1,0:T(8,128)(2,1)S(1)} %partial_preact.2), channel_id=1, replica_groups={{0,4,8,12},{1,5,9,13},{2,6,10,14},{3,7,11,15},{16,20,24,28},{17,21,25,2..., dimensions={0}, use_global_device_ids=true | all-gather | bytes 1146880 | tf_op jit(solution)/shard_map/all_gather | solution.py:410
  77.1 2.5 %quarter_grad.2 = bf16[4,400,128]{2,1,0:T(8,128)(2,1)S(1)} custom-call(s32[1]{0:T(128)} %bitcast.3.place, bf16[4096,112]{1,0:T(8,128)(2,1)S(1)} %all_gather.25.partials, bf16[256,1920]{1,0:T(8,128)(2,1)S(1)} %get-tuple-element.89.refs_0_, bf16[256,1920]{1,0:T(8,128)(2,1)S(1)} %collective-permute-done.10.refs_1_, ...), custom_call_target="tpu_custom_call" | custom-call | tf_op jit(solution)/shard_map/quarter_grad/pallas_call | solution.py:306
  79.6 31.1 %all_to_all.10.terms = bf16[4,400,128]{2,1,0:T(8,128)(2,1)S(1)} all-to-all(bf16[4,400,128]{2,1,0:T(8,128)(2,1)S(1)} %quarter_grad.2), channel_id=1, replica_groups={{0,1,2,3},{4,5,6,7},{8,9,10,11},{12,13,14,15},{16,17,18,19},{20,21,22,2..., dimensions={0} | all-to-all | bytes 819200 | tf_op jit(solution)/shard_map/all_to_all | solution.py:454
  110.7 3.4 %between.1 = (f32[392,128]{1,0:T(8,128)}, f32[392,128]{1,0:T(8,128)}, f32[400,128]{1,0:T(8,128)}, bf16[400,128]{1,0:T(8,128)(2,1)S(1)}) custom-call(f32[4]{0:T(128)S(1)} %reshape.60.scales, bf16[4,400,128]{2,1,0:T(8,128)(2,1)S(1)} %all_to_all.10.terms, f32[392,128]{1,0:T(8,128)} %bitcast.18, f32[392,128]{1,0:T(8,128)} %bitcast.19, ...), custom_call_target="tpu_custom_call" | custom-call | tf_op jit(solution)/shard_map/between/pallas_call | solution.py:373
  114.1 27.8 %conditional.3 = (f32[400,128]{1,0:T(8,128)}, bf16[1600,128]{1,0:T(8,128)(2,1)S(1)}) conditional(s32[]{:T(128)} %clamp.7, (f32[400,128]{1,0:T(8,128)}, bf16[400,128]{1,0:T(8,128)(2,1)S(1)}) %tuple.53, (f32[400,128]{1,0:T(8,128)}, bf16[400,128]{1,0:T(8,128)(2,1)S(1)}) %tuple.53, (f32[400,128]{1,0:T(8,128)}, ...), branch_computations={%region_5.6_spmd, %region_6.7_spmd, %region_7.8_spmd, %region_8.9_... | conditional | bytes 1331256 | solution.py:422
  114.1 3.0 %collective-permute-start.9 = (f32[400,128]{1,0:T(8,128)}, f32[400,128]{1,0:T(8,128)}, u32[]{:S(2)}, u32[]{:S(2)}) collective-permute-start(f32[400,128]{1,0:T(8,128)} %get-tuple-element.39), channel_id=1, source_target_pairs={{0,256},{16,272},{32,288},{48,304},{64,320},{80,336},{96,352},{112... | collective-permute-start | bytes 614408 | tf_op jit(solution)/shard_map/cond/branch_4_fun/ppermute | solution.py:60
  117.2 24.7 %all_gather.20 = bf16[1600,128]{1,0:T(8,128)(2,1)S(1)} all-gather(bf16[400,128]{1,0:T(8,128)(2,1)S(1)} %get-tuple-element.40), channel_id=1, replica_groups={{0,1,2,3},{4,5,6,7},{8,9,10,11},{12,13,14,15},{16,17,18,19},{20,21,22,2..., dimensions={0}, use_global_device_ids=true | all-gather | bytes 512000 | tf_op jit(solution)/shard_map/cond/branch_4_fun/all_gather | solution.py:410
  141.9 0.0 collective-permute-done.9
  141.9 2.6 %partial_preact.3 = bf16[1024,112]{1,0:T(8,128)(2,1)S(1)} custom-call(s32[1]{0:T(128)} %bitcast.3.place, bf16[1600,128]{1,0:T(8,128)(2,1)S(1)} %get-tuple-element.100.wires, bf16[256,1920]{1,0:T(8,128)(2,1)S(1)} %get-tuple-element.89.refs_0_, bf16[256,1920]{1,0:T(8,128)(2,1)S(1)} %collective-permute-done.10.refs_1_, ...), custom_call_target="tpu_custom_call" | custom-call | tf_op jit(solution)/shard_map/partial_preact/pallas_call | solution.py:247
  144.5 15.8 %all_gather.26.partials = bf16[4096,112]{1,0:T(8,128)(2,1)S(1)} all-gather(bf16[1024,112]{1,0:T(8,128)(2,1)S(1)} %partial_preact.3), channel_id=1, replica_groups={{0,4,8,12},{1,5,9,13},{2,6,10,14},{3,7,11,15},{16,20,24,28},{17,21,25,2..., dimensions={0}, use_global_device_ids=true | all-gather | bytes 1146880 | tf_op jit(solution)/shard_map/all_gather | solution.py:410
  160.4 2.8 %quarter_grad.3 = (bf16[4,400,128]{2,1,0:T(8,128)(2,1)S(1)}, f32[392,128]{1,0:T(8,128)S(1)}, f32[392,128]{1,0:T(8,128)S(1)}, f32[400,128]{1,0:T(8,128)S(1)}) custom-call(s32[1]{0:T(128)} %bitcast.3.place, bf16[4096,112]{1,0:T(8,128)(2,1)S(1)} %all_gather.26.partials, bf16[256,1920]{1,0:T(8,128)(2,1)S(1)} %get-tuple-element.89.refs_0_, ...), custom_call_target="tpu_custom_call" | custom-call | tf_op jit(solution)/shard_map/quarter_grad/pallas_call | solution.py:306
  163.2 24.1 %all_to_all.11.terms = bf16[4,400,128]{2,1,0:T(8,128)(2,1)S(1)} all-to-all(bf16[4,400,128]{2,1,0:T(8,128)(2,1)S(1)} %get-tuple-element.104), channel_id=1, replica_groups={{0,1,2,3},{4,5,6,7},{8,9,10,11},{12,13,14,15},{16,17,18,19},{20,21,22,2..., dimensions={0} | all-to-all | bytes 819200 | tf_op jit(solution)/shard_map/all_to_all | solution.py:454
  187.3 1.5 last.1
  (1 shorter events, 0.0 us)
Async XLA Ops:
  0.6 22.2 %copy-start = (f32[1,50176]{1,0:T(1,128)S(1)}, f32[1,50176]{1,0:T(1,128)}, u32[]{:S(2)}) copy-start(f32[1,50176]{1,0:T(1,128)} %param.19) | copy-start | bytes 602116
  4.7 55.3 %collective-permute-start.10 = (bf16[256,1920]{1,0:T(8,128)(2,1)}, bf16[256,1920]{1,0:T(8,128)(2,1)S(1)}, u32[]{:S(2)}, u32[]{:S(2)}) collective-permute-start(bf16[256,1920]{1,0:T(8,128)(2,1)} %get-tuple-element.90), channel_id=1, source_target_pairs={{0,4},{1,5},{2,6},{3,7},{4,8},{5,9},{6,10},{7,11},{8,12},{9,13},{1... | collective-permute-start | bytes 2949128 | tf_op jit(solution)/shard_map/ppermute | solution.py:55
  8.2 51.8 %collective-permute-start.13 = (bf16[256,1920]{1,0:T(8,128)(2,1)}, bf16[256,1920]{1,0:T(8,128)(2,1)}, u32[]{:S(2)}, u32[]{:S(2)}) collective-permute-start(bf16[256,1920]{1,0:T(8,128)(2,1)} %get-tuple-element.93), channel_id=1, source_target_pairs={{0,12},{1,13},{2,14},{3,15},{4,0},{5,1},{6,2},{7,3},{8,4},{9,5},{1... | collective-permute-start | bytes 2949128 | tf_op jit(solution)/shard_map/ppermute | solution.py:55
  13.9 46.0 %collective-permute-start.11 = (bf16[128,1920]{1,0:T(8,128)(2,1)}, bf16[128,1920]{1,0:T(8,128)(2,1)S(1)}, u32[]{:S(2)}, u32[]{:S(2)}) collective-permute-start(bf16[128,1920]{1,0:T(8,128)(2,1)} %get-tuple-element.91), channel_id=1, source_target_pairs={{0,8},{1,9},{2,10},{3,11},{4,12},{5,13},{6,14},{7,15},{8,0},{9,1},... | collective-permute-start | bytes 1474568 | tf_op jit(solution)/shard_map/ppermute | solution.py:55
  17.8 42.1 %collective-permute-start.12 = (bf16[128,1920]{1,0:T(8,128)(2,1)}, bf16[128,1920]{1,0:T(8,128)(2,1)S(1)}, u32[]{:S(2)}, u32[]{:S(2)}) collective-permute-start(bf16[128,1920]{1,0:T(8,128)(2,1)} %get-tuple-element.92), channel_id=1, source_target_pairs={{0,8},{1,9},{2,10},{3,11},{4,12},{5,13},{6,14},{7,15},{8,0},{9,1},... | collective-permute-start | bytes 1474568 | tf_op jit(solution)/shard_map/ppermute | solution.py:55
  52.0 8.0 %collective-permute-start.3 = (f32[400,128]{1,0:T(8,128)}, f32[400,128]{1,0:T(8,128)}, u32[]{:S(2)}, u32[]{:S(2)}) collective-permute-start(f32[400,128]{1,0:T(8,128)} %param.3), channel_id=1, source_target_pairs={{0,128},{16,144},{32,160},{48,176},{64,192},{80,208},{96,224},{112... | collective-permute-start | bytes 614408 | tf_op jit(solution)/shard_map/cond/branch_3_fun/ppermute | solution.py:60
  114.1 27.7 %collective-permute-start.9 = (f32[400,128]{1,0:T(8,128)}, f32[400,128]{1,0:T(8,128)}, u32[]{:S(2)}, u32[]{:S(2)}) collective-permute-start(f32[400,128]{1,0:T(8,128)} %get-tuple-element.39), channel_id=1, source_target_pairs={{0,256},{16,272},{32,288},{48,304},{64,320},{80,336},{96,352},{112... | collective-permute-start | bytes 614408 | tf_op jit(solution)/shard_map/cond/branch_4_fun/ppermute | solution.py:60
